TPU v7x, 128 devices: a whole 4x4x4 slice. The times are simulated.
128 devices in a mesh: gx: 8 (over y, z_hi), gy: 4 (over x), gz: 4 (over z_lo, core).
Axes of the slice: x: 4, y: 4, z: 4 (z_hi: 2, z_lo: 2; z = z_hi * 2 + z_lo), core: 2. Of those that a mesh axis runs over, the one named last changes fastest.
Arguments:
- pressure_now: float32 [256, 128, 512], P('gx', 'gy', 'gz'), may hold values from -6 to 6
- pressure_old: float32 [256, 128, 512], P('gx', 'gy', 'gz'), may hold values from -6 to 6
- cell_code: int32 [256, 128, 512], P('gx', 'gy', 'gz'), may hold values from 0 to 3
- surf_index: int32 [32, 2048], P(('gx', 'gz'), 'gy'), may hold values from -1 to 131071, as said below
- history: bfloat16 [540, 65536], P(None, ('gx', 'gz')), may hold values from -6 to 6
- dir_slot: int32 [512, 24], P(('gx', 'gz'), 'gy'), may hold values from -1 to 7, as said below
- delay: int32 [512, 24], P(('gx', 'gz'), 'gy'), may hold values from 0 to 32
- weights: bfloat16 [512, 24, 128, 128], P(('gx', 'gz'), 'gy'), may hold values from -0.0390625 to 0.0390625
Outputs:
- pressure_next: float32 [256, 128, 512], P('gx', 'gy', 'gz')
- pressure_prev: float32 [256, 128, 512], P('gx', 'gy', 'gz')
- far_field: float32 [512, 4096], P(('gx', 'gz'), 'gy')
Inputs may be any that keep to these rules, and one draw needn't show every extreme that they name: `surf_index`: in each brick's 512 slots the live ones come first; -1 marks an empty slot. `dir_slot`: within a panel block, the 6 entries of one direction group have their live entries first and -1 for dead ones.
All inputs are finite; a program needn't handle non-finite values.
Results may differ from a plain program's by a relative error of at most 0.0003.
Values may be sent and summed in bfloat16 or wider, within the bound.
A program may use at most 128 MiB of HBM per device.

v0:
```python
import functools

import jax
import jax.numpy as jnp
import numpy as np
from jax import lax
from jax.experimental import pallas as pl
from jax.experimental.pallas import tpu as pltpu
from jax.sharding import PartitionSpec as P

MESH = pl.DeviceIdType.MESH
F32 = jnp.float32
BF16 = jnp.bfloat16

STEPS = 4
CX, CY, CZ = 32, 32, 128
SLOT = 512
TW = 512
MAXOFF = 32
HOLD = 540
PB = 128
DB = 128
K_DEV = 6
BLOCKS = 16
ENTRIES = K_DEV * BLOCKS
PAIRS = ENTRIES // 2 + 4
TARGETS = 8
OWNERS = 32
ROWS = 16
NX_DEV, NY_DEV, NZ_DEV = 8, 4, 4
LOW, HIGH = 8, 40
PADROWS = 48


def coefficient_table():
    speeds = np.array([0.32, 0.26, 0.19, 0.11], np.float32).astype(np.float64)
    damping = np.array([0.0, 0.02, 0.08, 0.3], np.float32).astype(np.float64)
    here = (2.0 - 6.0 * speeds) / (1.0 + damping)
    before = -(1.0 - damping) / (1.0 + damping)
    around = speeds / (1.0 + damping)
    return [[float(np.float32(v)) for v in row] for row in (here, before, around)]


COEFFICIENTS = coefficient_table()


def hall_kernel(
    dir_ref, delay_ref, dirs_ref, surf_ref, hist_ref, now_ref, old_ref, code_ref, w_ref,
    next_ref, prev_ref, far_ref,
    field_a, field_b, codes, coef, ystage, zstage, xrecv, yrecv, zrecv,
    onehot, rounded, samp_send, samp_all, spad, lhs, wv,
    signal, trail, table, order, hist, part, core_recv, sums, totals, ring1, ring2, corr_out, corr_in,
    load_sem, halo_send, halo_recv, samp_ssem, samp_rsem,
    core_ssem, core_rsem, ring_send, ring_recv, corr_ssem, corr_rsem,
):
    fields = (field_a, field_b)
    gx, gy, gz = lax.axis_index("gx"), lax.axis_index("gy"), lax.axis_index("gz")
    y, z_hi = gx // 2, lax.rem(gx, 2)
    z_lo, core = gz // 2, lax.rem(gz, 2)
    z = z_hi * 2 + z_lo
    group = gx * 4 + gz
    is_owner = group == OWNERS - 1

    def place(yy, zz):
        return (yy * 2 + zz // 2, gy, lax.rem(zz, 2) * 2 + core)

    def ring_neighbour(axis, offset):
        if axis == "z":
            return place(y, lax.rem(z + offset, 4))
        return place(lax.rem(y + offset, 4), z)

    sibling = (gx, gy, z_lo * 2 + 1 - core)
    owner = (NX_DEV - 1, gy, NZ_DEV - 1)
    coords = (gx, gy, gz)
    extents = (NX_DEV, NY_DEV, NZ_DEV)

    def beside(axis, side):
        moved = list(coords)
        moved[axis] = coords[axis] + (1 if side else -1)
        return tuple(moved)

    def exists(axis, side):
        return coords[axis] < extents[axis] - 1 if side else coords[axis] > 0

    barrier = pltpu.get_barrier_semaphore()

    def greet(device):
        pl.semaphore_signal(barrier, inc=1, device_id=device, device_id_type=MESH)

    expected = jnp.int32(8)
    for axis in range(3):
        for side in range(2):
            @pl.when(exists(axis, side))
            def _():
                greet(beside(axis, side))
            expected = expected + exists(axis, side).astype(jnp.int32)
    greet(sibling)
    for axis in ("y", "z"):
        for offset in (1, 3):
            greet(ring_neighbour(axis, offset))
    for offset in range(1, NY_DEV):
        greet((gx, lax.rem(gy + offset, NY_DEV), gz))

    @pl.when(is_owner)
    def _():
        def greet_one(member, carry):
            greet((member // 4, gy, lax.rem(member, 4)))
            return carry
        lax.fori_loop(0, OWNERS - 1, greet_one, 0)

    expected = expected + jnp.where(is_owner, 0, 1)

    loads = [
        pltpu.make_async_copy(now_ref, field_a.at[pl.ds(1, CX), pl.ds(LOW, CY)], load_sem.at[0]),
        pltpu.make_async_copy(hist_ref, hist, load_sem.at[3]),
        pltpu.make_async_copy(w_ref, wv.at[pl.ds(0, ENTRIES)], load_sem.at[4]),
        pltpu.make_async_copy(code_ref, codes, load_sem.at[2]),
        pltpu.make_async_copy(old_ref, field_b.at[pl.ds(1, CX), pl.ds(LOW, CY)], load_sem.at[1]),
    ]
    for load in loads:
        load.start()

    lane = lax.broadcasted_iota(jnp.int32, (CY, CZ), 1)
    zero_plane = jnp.zeros((CY, CZ), F32)

    UNROLL = 4

    def over_planes(body, init):
        def chunk(i, carry):
            return body([i * UNROLL + u for u in range(UNROLL)], carry)
        return lax.fori_loop(0, CX // UNROLL, chunk, init)

    def take_faces(step, xs, planes, carry):
        low, high = carry
        for x, plane in zip(xs, planes):
            low = jnp.where(lane == x, pltpu.roll(plane, x, 1), low)
            high = jnp.where(lane == x, pltpu.roll(plane, x + 1, 1), high)
        for x, plane in zip(xs, planes):
            ystage[step, 0, pl.ds(x, 1), :] = plane[0:1, :]
            ystage[step, 1, pl.ds(x, 1), :] = plane[CY - 1:CY, :]
        return low, high

    def halo_copy(step, axis, side):
        current = step % 2
        if axis == 0:
            source = fields[current].at[CX if side else 1, pl.ds(LOW, CY)]
            target = xrecv.at[step, 1 - side]
        elif axis == 1:
            source, target = ystage.at[step, side], yrecv.at[step, 1 - side]
        else:
            source, target = zstage.at[step, side], zrecv.at[step, 1 - side]
        return pltpu.make_async_remote_copy(
            src_ref=source, dst_ref=target,
            send_sem=halo_send.at[step, axis, side],
            recv_sem=halo_recv.at[step, axis, 1 - side],
            device_id=beside(axis, side), device_id_type=MESH,
        )

    def halo_start(step):
        for axis in range(3):
            for side in range(2):
                @pl.when(exists(axis, side))
                def _():
                    halo_copy(step, axis, side).start()

    def halo_wait_send(step, axes=(0, 1, 2)):
        for axis in axes:
            for side in range(2):
                @pl.when(exists(axis, side))
                def _():
                    halo_copy(step, axis, side).wait_send()

    def halo_wait_recv(step, axes):
        for axis in axes:
            buffer = (xrecv, yrecv, zrecv)[axis]
            for side in range(2):
                @pl.when(exists(axis, side))
                def _():
                    halo_copy(step, axis, 1 - side).wait_recv()
                @pl.when(jnp.logical_not(exists(axis, side)))
                def _():
                    buffer[step, side] = zero_plane

    dirs = dirs_ref[...]
    targets = jnp.concatenate(
        [dirs[k:k + 1, :] for k in range(K_DEV)]
        + [jnp.full((1, PB - ENTRIES), -1, jnp.int32)], axis=1)
    targets = jnp.where(targets >= 0, targets, TARGETS).astype(F32)
    by_lane = jnp.broadcast_to(targets, (PB, PB))
    by_row = by_lane.T
    lanes = lax.broadcasted_iota(jnp.int32, (PB, PB), 1).astype(F32)
    rows = lax.broadcasted_iota(jnp.int32, (PB, PB), 0).astype(F32)

    def count(mask, axis):
        return jnp.sum(jnp.where(mask, 1.0, 0.0), axis=axis, keepdims=True)

    def even(amount):
        return 2.0 * jnp.floor(0.5 * (amount + 1.0))

    member = by_row == lanes
    along_lanes = count(member, 0)
    along_rows = count(by_lane == rows, 1)
    first_lanes = jnp.sum(jnp.where(rows < lanes, even(along_rows), 0.0), axis=0, keepdims=True)
    first_rows = jnp.sum(jnp.where(lanes < rows, even(along_lanes), 0.0), axis=1, keepdims=True)
    before = count(jnp.logical_and(by_lane == by_row, lanes < rows), 1)
    slot = before + jnp.sum(jnp.where(member, first_lanes, 0.0), axis=1, keepdims=True)
    taken = jnp.logical_and(slot == lanes, by_row < TARGETS)
    sequence = ENTRIES + jnp.sum(jnp.where(taken, rows - ENTRIES, 0.0), axis=0, keepdims=True)
    ends = jnp.where(along_lanes > 0, 0.5 * (first_lanes + even(along_lanes)), 0.0)
    opens = count(
        jnp.logical_and(jnp.logical_and(0.5 * first_rows == lanes, along_rows > 0), rows < TARGETS), 0)
    table[0:1, :] = sequence.astype(jnp.int32)
    table[1:2, :] = ends.astype(jnp.int32)
    table[2:3, :] = opens.astype(jnp.int32)
    table[3:8, :] = jnp.zeros((5, PB), jnp.int32)
    order_load = pltpu.make_async_copy(table, order, load_sem.at[7])
    order_load.start()

    loads[0].wait()

    def first_faces(xs, carry):
        return take_faces(0, xs, [field_a[x + 1, LOW:HIGH, :] for x in xs], carry)

    low, high = over_planes(first_faces, (zero_plane, zero_plane))
    zstage[0, 0] = low
    zstage[0, 1] = high

    pl.semaphore_wait(barrier, expected)
    halo_start(0)

    def core_copy(half):
        return pltpu.make_async_remote_copy(
            src_ref=part.at[pl.ds(half * 4, 4), :, :, 1 - core],
            dst_ref=core_recv.at[pl.ds(half * 4, 4)],
            send_sem=core_ssem.at[half], recv_sem=core_rsem.at[half],
            device_id=sibling, device_id_type=MESH,
        )

    loads[1].wait()

    def widen(block, carry):
        signal[block, HOLD:, :] = jnp.zeros((TW + MAXOFF - HOLD, PB), F32)
        return carry

    lax.fori_loop(0, BLOCKS, widen, 0)
    for block in range(BLOCKS):
        signal[block, :HOLD, :] = hist[:, block * PB:(block + 1) * PB].astype(F32)
    trail[0] = jnp.zeros((TW, DB), F32)
    order_load.wait()
    loads[2].wait()

    wv[ENTRIES] = jnp.zeros((PB, DB), BF16)

    def far_pair(p):
        windows, blocks = [], []
        for u in range(2):
            entry = jnp.clip(order[0, 2 * p + u], 0, ENTRIES)
            k = jnp.minimum(lax.shift_right_logical(entry, 4), K_DEV - 1)
            block = jnp.bitwise_and(entry, BLOCKS - 1)
            windows.append(signal[block, pl.ds(delay_ref[k, block], TW), :].astype(BF16))
            blocks.append(wv[jnp.where(entry < ENTRIES, block * K_DEV + k, ENTRIES)])
        term = jnp.dot(
            jnp.concatenate(windows, axis=1), jnp.concatenate(blocks, axis=0),
            preferred_element_type=F32)
        trail[p + 1] = term + trail[jnp.where(order[2, p] > 0, 0, p)]

    def far_pairs(first, amount):
        def chunk(i, carry):
            for u in range(2):
                far_pair(first + i * 2 + u)
            return carry
        lax.fori_loop(0, amount // 2, chunk, 0)

    def far_collect():
        for j in range(TARGETS):
            end = jnp.clip(order[1, j], 0, PAIRS)
            for quarter in range(4):
                found = trail[end, quarter * 128:(quarter + 1) * 128, :]
                part[j, quarter] = found.reshape(4, 2, ROWS, DB)

    far_pairs(0, 28)

    loads[3].wait()

    def plane_coefficients(xs, carry):
        for x in xs:
            code = codes[x]
            for index, values in enumerate(COEFFICIENTS):
                coef[index, x] = jnp.where(
                    code == 0, values[0],
                    jnp.where(code == 1, values[1], jnp.where(code == 2, values[2], values[3])),
                ).astype(F32)
        return carry

    over_planes(plane_coefficients, 0)
    cell = surf_ref[...]
    cell_row = lax.shift_right_arithmetic(cell, 7)
    cell_lane = jnp.bitwise_and(cell, CZ - 1)

    def build_onehot(i, carry):
        rows = lax.broadcasted_iota(jnp.int32, (32, SLOT), 0) + i * 32
        onehot[pl.ds(pl.multiple_of(i * 32, 32), 32), :] = jnp.where(
            rows == cell_row, 1.0, 0.0).astype(BF16)
        return carry

    lax.fori_loop(0, CX * CY // 32, build_onehot, 0)
    samp_send[...] = jnp.zeros_like(samp_send)
    spad[...] = jnp.zeros_like(spad)
    loads[4].wait()

    def leap(step):
        here_ref, other_ref = fields[step % 2], fields[1 - step % 2]
        last = step == STEPS - 1
        halo_wait_recv(step, (1, 2))

        def y_rows(xs, carry):
            rows = [(yrecv[step, 0, pl.ds(x, 1), :], yrecv[step, 1, pl.ds(x, 1), :]) for x in xs]
            for x, (low, high) in zip(xs, rows):
                here_ref[x + 1, LOW - 1:LOW, :] = low
                here_ref[x + 1, HIGH:HIGH + 1, :] = high
            return carry

        over_planes(y_rows, 0)
        z_low, z_high = zrecv[step, 0], zrecv[step, 1]

        def plane_step(xs, carry):
            planes = []
            for x in xs:
                here = here_ref[x + 1, LOW:HIGH, :]
                around = here_ref[x, LOW:HIGH, :] + here_ref[x + 2, LOW:HIGH, :]
                around = around + (
                    here_ref[x + 1, LOW - 1:HIGH - 1, :] + here_ref[x + 1, LOW + 1:HIGH + 1, :])
                below = jnp.where(
                    lane == 0, pltpu.roll(z_low, lax.rem(CZ - x, CZ), 1), pltpu.roll(here, 1, 1))
                above = jnp.where(
                    lane == CZ - 1, pltpu.roll(z_high, CZ - 1 - x, 1), pltpu.roll(here, CZ - 1, 1))
                around = around + (below + above)
                before = other_ref[x + 1, LOW:HIGH, :]
                planes.append(coef[0, x] * here + coef[1, x] * before + coef[2, x] * around)
            for x, new in zip(xs, planes):
                other_ref[x + 1, LOW:HIGH, :] = new
                rounded[pl.ds(pl.multiple_of(x * CY, CY), CY), :] = new.astype(BF16)
            if last:
                return carry
            return take_faces(step + 1, xs, planes, carry)

        def inner(i, carry):
            return plane_step([1 + i * 5 + u for u in range(5)], carry)

        carry = lax.fori_loop(
            0, (CX - 2) // 5, inner, 0 if last else (zero_plane, zero_plane))
        halo_wait_recv(step, (0,))
        if step > 0:
            halo_wait_send(step - 1, (0,))
        here_ref[0, LOW:HIGH, :] = xrecv[step, 0]
        here_ref[CX + 1, LOW:HIGH, :] = xrecv[step, 1]
        carry = plane_step([0, CX - 1], carry)
        if not last:
            zstage[step + 1, 0], zstage[step + 1, 1] = carry
            halo_start(step + 1)

    def sample(step):
        picked = lax.dot_general(
            rounded[...], onehot[...], (((0,), (0,)), ((), ())), preferred_element_type=F32)
        level = lax.broadcasted_iota(jnp.int32, (CZ, SLOT), 0)
        values = jnp.sum(jnp.where(level == cell_lane, picked, 0.0), axis=0, keepdims=True)
        samp_send[4 + step:5 + step, :] = values

    axes = (("z", "y"), ("y", "z"))

    def index_on(axis):
        return z if axis == "z" else y

    def ring_copy(half, stage, kind, way):
        axis = axes[half][stage]
        place_now = index_on(axis)
        step_to = 1 if way == 0 else 3
        chunk = lax.rem(place_now + (2 if kind == 0 else step_to), 4)
        part = pl.ds(0 if (kind == 1) == (way == 1) else 2, 2)
        if stage == 0:
            source, target = sums.at[half, chunk, part], ring1.at[half, kind, way]
        else:
            source, target = totals.at[half, chunk, part], ring2.at[half, kind, way]
        return pltpu.make_async_remote_copy(
            src_ref=source, dst_ref=target,
            send_sem=ring_send.at[half, stage, kind, way],
            recv_sem=ring_recv.at[half, stage, kind, way],
            device_id=ring_neighbour(axis, step_to), device_id_type=MESH,
        )

    def core_finish(half):
        core_copy(half).wait_recv()

        def add(i, carry):
            yy, zz = i // 4, lax.rem(i, 4)
            total = part[half * 4:half * 4 + 4, yy, zz, core] + core_recv[half * 4:half * 4 + 4, yy, zz]
            if half == 0:
                sums[0, zz, yy] = total
            else:
                sums[1, yy, zz] = total
            return carry

        lax.fori_loop(0, 16, add, 0)

    def ring_begin(half, stage):
        for kind in (0, 1):
            for way in (0, 1):
                ring_copy(half, stage, kind, way).start()

    def ring_forward(half, stage):
        held = sums if stage == 0 else totals
        arrived = ring1 if stage == 0 else ring2
        place_now = index_on(axes[half][stage])
        for way in (0, 1):
            ring_copy(half, stage, 0, way).wait_recv()
            chunk = lax.rem(place_now + (1 if way == 0 else 3), 4)
            first = 0 if way == 0 else 2
            held[half, chunk, first:first + 2] = (
                held[half, chunk, first:first + 2] + arrived[half, 0, way])
            ring_copy(half, stage, 2, way).start()

    def ring_end(half, stage):
        held = sums if stage == 0 else totals
        arrived = ring1 if stage == 0 else ring2
        place_now = index_on(axes[half][stage])
        for kind in (1, 2):
            for way in (0, 1):
                ring_copy(half, stage, kind, way).wait_recv()
        first = held[half, place_now, 0:2] + (arrived[half, 2, 0] + arrived[half, 1, 1])
        second = held[half, place_now, 2:4] + (arrived[half, 1, 0] + arrived[half, 2, 1])
        return first, second

    leap(0)
    sample(0)
    far_pairs(28, PAIRS - 28)
    far_collect()
    for half in range(2):
        core_copy(half).start()
    leap(1)
    sample(1)
    for half in range(2):
        core_finish(half)
        ring_begin(half, 0)
    leap(2)
    save_prev = pltpu.make_async_copy(
        field_b.at[pl.ds(1, CX), pl.ds(LOW, CY)], prev_ref, load_sem.at[5])
    save_prev.start()
    sample(2)
    for half in range(2):
        ring_forward(half, 0)
    leap(3)
    save_next = pltpu.make_async_copy(
        field_a.at[pl.ds(1, CX), pl.ds(LOW, CY)], next_ref, load_sem.at[6])
    save_next.start()
    sample(3)

    def samp_copy(offset):
        return pltpu.make_async_remote_copy(
            src_ref=samp_send, dst_ref=samp_all.at[gy],
            send_sem=samp_ssem.at[offset - 1], recv_sem=samp_rsem.at[offset - 1],
            device_id=(gx, lax.rem(gy + offset, NY_DEV), gz), device_id_type=MESH,
        )

    def samp_arrival(offset):
        return pltpu.make_async_remote_copy(
            src_ref=samp_send, dst_ref=samp_all.at[lax.rem(gy + NY_DEV - offset, NY_DEV)],
            send_sem=samp_ssem.at[offset - 1], recv_sem=samp_rsem.at[offset - 1],
            device_id=(gx, lax.rem(gy + offset, NY_DEV), gz), device_id_type=MESH,
        )

    for offset in range(1, NY_DEV):
        samp_copy(offset).start()
    samp_all[gy] = samp_send[...]
    for half in range(2):
        first, second = ring_end(half, 0)
        totals[half, 0:2] = first
        totals[half, 2:4] = second
        ring_begin(half, 1)
    for offset in range(1, NY_DEV):
        samp_arrival(offset).wait_recv()
    for brick in range(NY_DEV):
        for i in range(SLOT // PB):
            spad[brick * (SLOT // PB) + i, 32:40, :] = samp_all[brick, :, i * PB:(i + 1) * PB]

    row = lax.broadcasted_iota(jnp.int32, (8, PB), 0)

    def entry_rows(block, carry):
        for entry in range(K_DEV):
            offset = delay_ref[entry, block]
            target = dir_ref[entry, block]
            early = spad[block, pl.ds(offset + 4, 8), :]
            late = spad[block, pl.ds(offset, 8), :]
            pair = jnp.where(row < 4, early, late)
            pieces = []
            for i in range(TARGETS // 2):
                wanted = jnp.where(row < 4, 2 * i, 2 * i + 1)
                pieces.append(jnp.where(wanted == target, pair, 0.0))
            lhs[:, pl.ds(pl.multiple_of((block * K_DEV + entry) * PB, PB), PB)] = (
                jnp.concatenate(pieces, axis=0).astype(BF16))
        return carry

    lax.fori_loop(0, BLOCKS, entry_rows, 0)
    for half in range(2):
        ring_forward(half, 1)
    flat_weights = wv[:ENTRIES].reshape(BLOCKS * K_DEV * PB, DB)
    correction = jnp.dot(lhs[...], flat_weights, preferred_element_type=F32)
    corr_out[...] = correction

    def corr_copy(member):
        return pltpu.make_async_remote_copy(
            src_ref=corr_out, dst_ref=corr_in.at[member],
            send_sem=corr_ssem, recv_sem=corr_rsem.at[member],
            device_id=owner, device_id_type=MESH,
        )

    @pl.when(jnp.logical_not(is_owner))
    def _():
        corr_copy(group).start()

    for half in range(2):
        first, second = ring_end(half, 1)
        for j in range(4):
            columns = slice((half * 4 + j) * DB, (half * 4 + j + 1) * DB)
            far_ref[:, columns] = first[j] if j < 2 else second[j - 2]

    @pl.when(is_owner)
    def _():
        def arrive(member, total):
            corr_copy(member).wait_recv()
            return total + corr_in[member]

        total = lax.fori_loop(0, OWNERS - 1, arrive, corr_out[...])
        for j in range(TARGETS):
            piece = total[(j // 2) * 8:(j // 2) * 8 + 8, :]
            if j % 2 == 0:
                piece = pltpu.roll(piece, 4, 0)
            columns = slice(j * DB, (j + 1) * DB)
            far_ref[8:16, columns] = far_ref[8:16, columns] + jnp.where(row >= 4, piece, 0.0)

    for step in range(STEPS):
        halo_wait_send(step, (0, 1, 2) if step == STEPS - 1 else (1, 2))
    for half in range(2):
        core_copy(half).wait_send()
        for stage in range(2):
            for kind in range(3):
                for way in range(2):
                    ring_copy(half, stage, kind, way).wait_send()
    for offset in range(1, NY_DEV):
        samp_copy(offset).wait_send()

    @pl.when(jnp.logical_not(is_owner))
    def _():
        corr_copy(group).wait_send()

    save_prev.wait()
    save_next.wait()


def hall(dirs, delays, surf_index, now, old, code, history, weights):
    any_space = pl.BlockSpec(memory_space=pl.ANY)
    smem = pl.BlockSpec(memory_space=pltpu.SMEM)
    vmem = pl.BlockSpec(memory_space=pltpu.VMEM)
    dma = pltpu.SemaphoreType.DMA
    brick = jax.ShapeDtypeStruct((CX, CY, CZ), F32)
    return pl.pallas_call(
        hall_kernel,
        out_shape=(brick, brick, jax.ShapeDtypeStruct((ROWS, TARGETS * DB), F32)),
        in_specs=[smem, smem, vmem, vmem] + [any_space] * 5,
        out_specs=(any_space, any_space, vmem),
        scratch_shapes=[
            pltpu.VMEM((CX + 2, PADROWS, CZ), F32),
            pltpu.VMEM((CX + 2, PADROWS, CZ), F32),
            pltpu.VMEM((CX, CY, CZ), jnp.int32),
            pltpu.VMEM((3, CX, CY, CZ), F32),
            pltpu.VMEM((STEPS, 2, CX, CZ), F32),
            pltpu.VMEM((STEPS, 2, CY, CZ), F32),
            pltpu.VMEM((STEPS, 2, CY, CZ), F32),
            pltpu.VMEM((STEPS, 2, CX, CZ), F32),
            pltpu.VMEM((STEPS, 2, CY, CZ), F32),
            pltpu.VMEM((CX * CY, SLOT), BF16),
            pltpu.VMEM((CX * CY, CZ), BF16),
            pltpu.VMEM((8, SLOT), F32),
            pltpu.VMEM((NY_DEV, 8, SLOT), F32),
            pltpu.VMEM((BLOCKS, 48, PB), F32),
            pltpu.VMEM((32, BLOCKS * K_DEV * PB), BF16),
            pltpu.VMEM((ENTRIES + 1, PB, DB), BF16),
            pltpu.VMEM((BLOCKS, TW + MAXOFF, PB), F32),
            pltpu.VMEM((PAIRS + 1, TW, DB), F32),
            pltpu.VMEM((8, PB), jnp.int32),
            pltpu.SMEM((8, PB), jnp.int32),
            pltpu.VMEM((HOLD, BLOCKS * PB), BF16),
            pltpu.VMEM((TARGETS, 4, 4, 2, ROWS, DB), F32),
            pltpu.VMEM((TARGETS, 4, 4, ROWS, DB), F32),
            pltpu.VMEM((2, 4, 4, 4, ROWS, DB), F32),
            pltpu.VMEM((2, 4, 4, ROWS, DB), F32),
            pltpu.VMEM((2, 3, 2, 2, 4, ROWS, DB), F32),
            pltpu.VMEM((2, 3, 2, 2, ROWS, DB), F32),
            pltpu.VMEM((32, DB), F32),
            pltpu.VMEM((OWNERS, 32, DB), F32),
            dma((8,)),
            dma((STEPS, 3, 2)), dma((STEPS, 3, 2)),
            dma((3,)), dma((3,)),
            dma((2,)), dma((2,)),
            dma((2, 2, 3, 2)), dma((2, 2, 3, 2)),
            dma, dma((OWNERS,)),
        ],
        compiler_params=pltpu.CompilerParams(
            collective_id=0, has_side_effects=True, vmem_limit_bytes=58 * 1024 * 1024),
    )(dirs, delays, dirs, surf_index, history, now, old, code, weights)


def save_kernel(*refs):
    sources, targets, held, sems = refs[:3], refs[3:6], refs[6:9], refs[9]
    arrivals = [pltpu.make_async_copy(sources[i], held[i], sems.at[0, i]) for i in range(3)]
    leaves = [pltpu.make_async_copy(held[i], targets[i], sems.at[1, i]) for i in range(3)]
    for copy in arrivals:
        copy.start()
    for arrival, leave in zip(arrivals, leaves):
        arrival.wait()
        leave.start()
    for copy in leaves:
        copy.wait()


def save(arrays):
    any_space = pl.BlockSpec(memory_space=pl.ANY)
    return pl.pallas_call(
        save_kernel,
        out_shape=tuple(jax.ShapeDtypeStruct(a.shape, a.dtype) for a in arrays),
        in_specs=[any_space] * 3,
        out_specs=(any_space,) * 3,
        scratch_shapes=[pltpu.VMEM(a.shape, a.dtype) for a in arrays]
        + [pltpu.SemaphoreType.DMA((2, 3))],
    )(*arrays)


def shards(pressure_now, pressure_old, cell_code, surf_index, history, dir_slot, delay, weights):
    flat_weights = weights.reshape(BLOCKS * K_DEV, PB, DB)
    return save(hall(
        dir_slot.T, delay.T, surf_index, pressure_now, pressure_old, cell_code, history,
        flat_weights))


def solution(mesh):
    return jax.shard_map(
        shards,
        mesh=mesh,
        in_specs=(
            P("gx", "gy", "gz"),
            P("gx", "gy", "gz"),
            P("gx", "gy", "gz"),
            P(("gx", "gz"), "gy"),
            P(None, ("gx", "gz")),
            P(("gx", "gz"), "gy"),
            P(("gx", "gz"), "gy"),
            P(("gx", "gz"), "gy", None, None),
        ),
        out_specs=(P("gx", "gy", "gz"), P("gx", "gy", "gz"), P(("gx", "gz"), "gy")),
        check_vma=False,
    )
```

profile of v0, /device:TPU:0, one launch (start us, length us, event | category | flops | bytes accessed | tf_op | source)
XLA Modules:
  0.0 43.6 jit_solution(8898066889284466841)
XLA Ops:
  0.6 40.9 %shard_map.103 = (f32[32,32,128]{2,1,0:T(8,128)}, f32[32,32,128]{2,1,0:T(8,128)}, f32[16,1024]{1,0:T(8,128)}) custom-call(s32[6,16]{1,0:T(8,128)} %bitcast.4, s32[6,16]{1,0:T(8,128)} %bitcast.6, s32[6,16]{1,0:T(8,128)} %bitcast.5, s32[1,512]{1,0:T(1,128)} %surf_ref.1, bf16[540,2048]{1,0:T(8,128)(2,1)} %hist_ref.1, f32[32,32,128]{2,1,0:T(8,128)} %now_ref.1, ...), custom_call_target="tpu_custom_call" | custom-call | tf_op jit(solution)/shard_map/pallas_call | solution.py:565
  41.5 2.1 %shard_map.104 = (f32[32,32,128]{2,1,0:T(8,128)}, f32[32,32,128]{2,1,0:T(8,128)}, f32[16,1024]{1,0:T(8,128)}) custom-call(f32[32,32,128]{2,1,0:T(8,128)} %get-tuple-element.6.refs_0_, f32[32,32,128]{2,1,0:T(8,128)} %get-tuple-element.7.refs_1_, f32[16,1024]{1,0:T(8,128)} %get-tuple-element.8.refs_2_), custom_call_target="tpu_custom_call" | custom-call | tf_op jit(solution)/shard_map/pallas_call | solution.py:627
where the time goes:
time: 43.8 us; the launch traced here: 43.6 us
  Pallas kernels  43 us (98%)
  between operations  0.64 us (1%)
    pallas_call x1, Pallas kernels, hall(): pl.pallas_call(hall_kernel, out_shape=(brick, brick, jax.ShapeDtypeStruct...  40.9 us
    pallas_call x1, Pallas kernels, save(): pl.pallas_call(save_kernel, out_shape=tuple((jax.ShapeDtypeStruct(a.shape...  2.07 us

commit v1 on v0

--- a/solution.py
+++ b/solution.py
@@ -123,12 +123,10 @@
     lane = lax.broadcasted_iota(jnp.int32, (CY, CZ), 1)
     zero_plane = jnp.zeros((CY, CZ), F32)
 
-    UNROLL = 4
-
-    def over_planes(body, init):
+    def over_planes(body, init, unroll=8):
         def chunk(i, carry):
-            return body([i * UNROLL + u for u in range(UNROLL)], carry)
-        return lax.fori_loop(0, CX // UNROLL, chunk, init)
+            return body([i * unroll + u for u in range(unroll)], carry)
+        return lax.fori_loop(0, CX // unroll, chunk, init)
 
     def take_faces(step, xs, planes, carry):
         low, high = carry
@@ -180,6 +178,18 @@
                 @pl.when(jnp.logical_not(exists(axis, side)))
                 def _():
                     buffer[step, side] = zero_plane
+
+    loads[0].wait()
+
+    def first_faces(xs, carry):
+        return take_faces(0, xs, [field_a[x + 1, LOW:HIGH, :] for x in xs], carry)
+
+    low, high = over_planes(first_faces, (zero_plane, zero_plane))
+    zstage[0, 0] = low
+    zstage[0, 1] = high
+
+    pl.semaphore_wait(barrier, expected)
+    halo_start(0)
 
     dirs = dirs_ref[...]
     targets = jnp.concatenate(
@@ -216,18 +226,6 @@
     order_load = pltpu.make_async_copy(table, order, load_sem.at[7])
     order_load.start()
 
-    loads[0].wait()
-
-    def first_faces(xs, carry):
-        return take_faces(0, xs, [field_a[x + 1, LOW:HIGH, :] for x in xs], carry)
-
-    low, high = over_planes(first_faces, (zero_plane, zero_plane))
-    zstage[0, 0] = low
-    zstage[0, 1] = high
-
-    pl.semaphore_wait(barrier, expected)
-    halo_start(0)
-
     def core_copy(half):
         return pltpu.make_async_remote_copy(
             src_ref=part.at[pl.ds(half * 4, 4), :, :, 1 - core],
@@ -264,12 +262,12 @@
             preferred_element_type=F32)
         trail[p + 1] = term + trail[jnp.where(order[2, p] > 0, 0, p)]
 
-    def far_pairs(first, amount):
+    def far_pairs(first, amount, unroll):
         def chunk(i, carry):
-            for u in range(2):
-                far_pair(first + i * 2 + u)
+            for u in range(unroll):
+                far_pair(first + i * unroll + u)
             return carry
-        lax.fori_loop(0, amount // 2, chunk, 0)
+        lax.fori_loop(0, amount // unroll, chunk, 0)
 
     def far_collect():
         for j in range(TARGETS):
@@ -278,7 +276,10 @@
                 found = trail[end, quarter * 128:(quarter + 1) * 128, :]
                 part[j, quarter] = found.reshape(4, 2, ROWS, DB)
 
-    far_pairs(0, 28)
+    def core_start():
+        far_collect()
+        for half in range(2):
+            core_copy(half).start()
 
     loads[3].wait()
 
@@ -298,12 +299,12 @@
     cell_lane = jnp.bitwise_and(cell, CZ - 1)
 
     def build_onehot(i, carry):
-        rows = lax.broadcasted_iota(jnp.int32, (32, SLOT), 0) + i * 32
-        onehot[pl.ds(pl.multiple_of(i * 32, 32), 32), :] = jnp.where(
+        rows = lax.broadcasted_iota(jnp.int32, (128, SLOT), 0) + i * 128
+        onehot[pl.ds(pl.multiple_of(i * 128, 128), 128), :] = jnp.where(
             rows == cell_row, 1.0, 0.0).astype(BF16)
         return carry
 
-    lax.fori_loop(0, CX * CY // 32, build_onehot, 0)
+    lax.fori_loop(0, CX * CY // 128, build_onehot, 0)
     samp_send[...] = jnp.zeros_like(samp_send)
     spad[...] = jnp.zeros_like(spad)
     loads[4].wait()
@@ -320,7 +321,7 @@
                 here_ref[x + 1, HIGH:HIGH + 1, :] = high
             return carry
 
-        over_planes(y_rows, 0)
+        over_planes(y_rows, 0, 16)
         z_low, z_high = zrecv[step, 0], zrecv[step, 1]
 
         def plane_step(xs, carry):
@@ -345,10 +346,10 @@
             return take_faces(step + 1, xs, planes, carry)
 
         def inner(i, carry):
-            return plane_step([1 + i * 5 + u for u in range(5)], carry)
+            return plane_step([1 + i * 10 + u for u in range(10)], carry)
 
         carry = lax.fori_loop(
-            0, (CX - 2) // 5, inner, 0 if last else (zero_plane, zero_plane))
+            0, (CX - 2) // 10, inner, 0 if last else (zero_plane, zero_plane))
         halo_wait_recv(step, (0,))
         if step > 0:
             halo_wait_send(step - 1, (0,))
@@ -391,16 +392,14 @@
     def core_finish(half):
         core_copy(half).wait_recv()
 
-        def add(i, carry):
-            yy, zz = i // 4, lax.rem(i, 4)
-            total = part[half * 4:half * 4 + 4, yy, zz, core] + core_recv[half * 4:half * 4 + 4, yy, zz]
-            if half == 0:
-                sums[0, zz, yy] = total
-            else:
-                sums[1, yy, zz] = total
-            return carry
-
-        lax.fori_loop(0, 16, add, 0)
+        for yy in range(4):
+            for zz in range(4):
+                total = (part[half * 4:half * 4 + 4, yy, zz, core]
+                         + core_recv[half * 4:half * 4 + 4, yy, zz])
+                if half == 0:
+                    sums[0, zz, yy] = total
+                else:
+                    sums[1, yy, zz] = total
 
     def ring_begin(half, stage):
         for kind in (0, 1):
@@ -430,12 +429,11 @@
         second = held[half, place_now, 2:4] + (arrived[half, 1, 0] + arrived[half, 2, 1])
         return first, second
 
+    far_pairs(0, 28, 14)
     leap(0)
     sample(0)
-    far_pairs(28, PAIRS - 28)
-    far_collect()
-    for half in range(2):
-        core_copy(half).start()
+    far_pairs(28, PAIRS - 28, 12)
+    core_start()
     leap(1)
     sample(1)
     for half in range(2):
@@ -484,22 +482,25 @@
 
     row = lax.broadcasted_iota(jnp.int32, (8, PB), 0)
 
-    def entry_rows(block, carry):
-        for entry in range(K_DEV):
-            offset = delay_ref[entry, block]
-            target = dir_ref[entry, block]
-            early = spad[block, pl.ds(offset + 4, 8), :]
-            late = spad[block, pl.ds(offset, 8), :]
-            pair = jnp.where(row < 4, early, late)
-            pieces = []
-            for i in range(TARGETS // 2):
-                wanted = jnp.where(row < 4, 2 * i, 2 * i + 1)
-                pieces.append(jnp.where(wanted == target, pair, 0.0))
-            lhs[:, pl.ds(pl.multiple_of((block * K_DEV + entry) * PB, PB), PB)] = (
-                jnp.concatenate(pieces, axis=0).astype(BF16))
+    def entry_rows(i, carry):
+        held = []
+        for block in [i * 4 + u for u in range(4)]:
+            for entry in range(K_DEV):
+                offset = delay_ref[entry, block]
+                target = dir_ref[entry, block]
+                early = spad[block, pl.ds(offset + 4, 8), :]
+                late = spad[block, pl.ds(offset, 8), :]
+                pair = jnp.where(row < 4, early, late)
+                pieces = []
+                for k in range(TARGETS // 2):
+                    wanted = jnp.where(row < 4, 2 * k, 2 * k + 1)
+                    pieces.append(jnp.where(wanted == target, pair, 0.0))
+                held.append(jnp.concatenate(pieces, axis=0).astype(BF16))
+        width = 4 * K_DEV * PB
+        lhs[:, pl.ds(pl.multiple_of(i * width, width), width)] = jnp.concatenate(held, axis=1)
         return carry
 
-    lax.fori_loop(0, BLOCKS, entry_rows, 0)
+    lax.fori_loop(0, BLOCKS // 4, entry_rows, 0)
     for half in range(2):
         ring_forward(half, 1)
     flat_weights = wv[:ENTRIES].reshape(BLOCKS * K_DEV * PB, DB)
@@ -525,11 +526,14 @@
 
     @pl.when(is_owner)
     def _():
-        def arrive(member, total):
+        def arrive(member, carry):
             corr_copy(member).wait_recv()
-            return total + corr_in[member]
-
-        total = lax.fori_loop(0, OWNERS - 1, arrive, corr_out[...])
+            return carry
+
+        lax.fori_loop(0, OWNERS - 1, arrive, 0)
+        total = corr_out[...]
+        for member in range(OWNERS - 1):
+            total = total + corr_in[member]
         for j in range(TARGETS):
             piece = total[(j // 2) * 8:(j // 2) * 8 + 8, :]
             if j % 2 == 0:

time: 43.8 us -> 39.3 us (0.90)
  Pallas kernels: 43 us -> 38.5 us
    pallas_call x1, Pallas kernels: 40.9 us -> 36.5 us  [hall(): pl.pallas_call(hall_kernel, out_shape=(brick, brick, jax.ShapeDtypeStruct...]
where the time goes in v1:
time: 39.3 us; the launch traced here: 39.2 us
  Pallas kernels  38.5 us (98%)
  between operations  0.64 us (2%)
    pallas_call x1, Pallas kernels, hall(): pl.pallas_call(hall_kernel, out_shape=(brick, brick, jax.ShapeDtypeStruct...  36.5 us
    pallas_call x1, Pallas kernels, save(): pl.pallas_call(save_kernel, out_shape=tuple((jax.ShapeDtypeStruct(a.shape...  2.07 us

profile of v1, /device:TPU:0, one launch (start us, length us, event | category | flops | bytes accessed | tf_op | source)
XLA Modules:
  0.0 39.2 jit_solution(17820256354730714703)
XLA Ops:
  0.6 36.5 %shard_map.103 = (f32[32,32,128]{2,1,0:T(8,128)}, f32[32,32,128]{2,1,0:T(8,128)}, f32[16,1024]{1,0:T(8,128)}) custom-call(s32[6,16]{1,0:T(8,128)} %bitcast.4, s32[6,16]{1,0:T(8,128)} %bitcast.6, s32[6,16]{1,0:T(8,128)} %bitcast.5, s32[1,512]{1,0:T(1,128)} %surf_ref.1, bf16[540,2048]{1,0:T(8,128)(2,1)} %hist_ref.1, f32[32,32,128]{2,1,0:T(8,128)} %now_ref.1, ...), custom_call_target="tpu_custom_call" | custom-call | tf_op jit(solution)/shard_map/pallas_call | solution.py:569
  37.1 2.1 %shard_map.104 = (f32[32,32,128]{2,1,0:T(8,128)}, f32[32,32,128]{2,1,0:T(8,128)}, f32[16,1024]{1,0:T(8,128)}) custom-call(f32[32,32,128]{2,1,0:T(8,128)} %get-tuple-element.6.refs_0_, f32[32,32,128]{2,1,0:T(8,128)} %get-tuple-element.7.refs_1_, f32[16,1024]{1,0:T(8,128)} %get-tuple-element.8.refs_2_), custom_call_target="tpu_custom_call" | custom-call | tf_op jit(solution)/shard_map/pallas_call | solution.py:631

commit v2 on v1

--- a/solution.py
+++ b/solution.py
@@ -48,10 +48,10 @@
     dir_ref, delay_ref, dirs_ref, surf_ref, hist_ref, now_ref, old_ref, code_ref, w_ref,
     next_ref, prev_ref, far_ref,
     field_a, field_b, codes, coef, ystage, zstage, xrecv, yrecv, zrecv,
-    onehot, rounded, samp_send, samp_all, spad, lhs, wv,
-    signal, trail, table, order, hist, part, core_recv, sums, totals, ring1, ring2, corr_out, corr_in,
+    onehot, rounded, samp_send, samp_all, last_send, last_all, spad, lhs, last_lhs, wv,
+    signal, trail, table, order, hist, part, core_recv, sums, totals, ring1, ring2, corr_out, corr_in, last_out, last_in,
     load_sem, halo_send, halo_recv, samp_ssem, samp_rsem,
-    core_ssem, core_rsem, ring_send, ring_recv, corr_ssem, corr_rsem,
+    core_ssem, core_rsem, ring_send, ring_recv, corr_ssem, corr_rsem, last_ssem, last_rsem,
 ):
     fields = (field_a, field_b)
     gx, gy, gz = lax.axis_index("gx"), lax.axis_index("gy"), lax.axis_index("gz")
@@ -340,7 +340,7 @@
                 planes.append(coef[0, x] * here + coef[1, x] * before + coef[2, x] * around)
             for x, new in zip(xs, planes):
                 other_ref[x + 1, LOW:HIGH, :] = new
-                rounded[pl.ds(pl.multiple_of(x * CY, CY), CY), :] = new.astype(BF16)
+                rounded[step % 2, pl.ds(x * CY if isinstance(x, int) else pl.multiple_of(x * CY, CY), CY), :] = new.astype(BF16)
             if last:
                 return carry
             return take_faces(step + 1, xs, planes, carry)
@@ -362,10 +362,13 @@
 
     def sample(step):
         picked = lax.dot_general(
-            rounded[...], onehot[...], (((0,), (0,)), ((), ())), preferred_element_type=F32)
+            rounded[step % 2], onehot[...], (((0,), (0,)), ((), ())), preferred_element_type=F32)
         level = lax.broadcasted_iota(jnp.int32, (CZ, SLOT), 0)
         values = jnp.sum(jnp.where(level == cell_lane, picked, 0.0), axis=0, keepdims=True)
-        samp_send[4 + step:5 + step, :] = values
+        if step < STEPS - 1:
+            samp_send[4 + step:5 + step, :] = values
+        else:
+            last_send[...] = jnp.broadcast_to(values, (8, SLOT))
 
     axes = (("z", "y"), ("y", "z"))
 
@@ -429,58 +432,29 @@
         second = held[half, place_now, 2:4] + (arrived[half, 1, 0] + arrived[half, 2, 1])
         return first, second
 
-    far_pairs(0, 28, 14)
-    leap(0)
-    sample(0)
-    far_pairs(28, PAIRS - 28, 12)
-    core_start()
-    leap(1)
-    sample(1)
-    for half in range(2):
-        core_finish(half)
-        ring_begin(half, 0)
-    leap(2)
-    save_prev = pltpu.make_async_copy(
-        field_b.at[pl.ds(1, CX), pl.ds(LOW, CY)], prev_ref, load_sem.at[5])
-    save_prev.start()
-    sample(2)
-    for half in range(2):
-        ring_forward(half, 0)
-    leap(3)
-    save_next = pltpu.make_async_copy(
-        field_a.at[pl.ds(1, CX), pl.ds(LOW, CY)], next_ref, load_sem.at[6])
-    save_next.start()
-    sample(3)
-
-    def samp_copy(offset):
+    def samp_copy(last, offset, arriving=False):
+        source, target = (last_send, last_all) if last else (samp_send, samp_all)
+        slot = lax.rem(gy + NY_DEV - offset, NY_DEV) if arriving else gy
         return pltpu.make_async_remote_copy(
-            src_ref=samp_send, dst_ref=samp_all.at[gy],
-            send_sem=samp_ssem.at[offset - 1], recv_sem=samp_rsem.at[offset - 1],
+            src_ref=source, dst_ref=target.at[slot],
+            send_sem=samp_ssem.at[last, offset - 1], recv_sem=samp_rsem.at[last, offset - 1],
             device_id=(gx, lax.rem(gy + offset, NY_DEV), gz), device_id_type=MESH,
         )
 
-    def samp_arrival(offset):
-        return pltpu.make_async_remote_copy(
-            src_ref=samp_send, dst_ref=samp_all.at[lax.rem(gy + NY_DEV - offset, NY_DEV)],
-            send_sem=samp_ssem.at[offset - 1], recv_sem=samp_rsem.at[offset - 1],
-            device_id=(gx, lax.rem(gy + offset, NY_DEV), gz), device_id_type=MESH,
-        )
-
-    for offset in range(1, NY_DEV):
-        samp_copy(offset).start()
-    samp_all[gy] = samp_send[...]
-    for half in range(2):
-        first, second = ring_end(half, 0)
-        totals[half, 0:2] = first
-        totals[half, 2:4] = second
-        ring_begin(half, 1)
-    for offset in range(1, NY_DEV):
-        samp_arrival(offset).wait_recv()
-    for brick in range(NY_DEV):
-        for i in range(SLOT // PB):
-            spad[brick * (SLOT // PB) + i, 32:40, :] = samp_all[brick, :, i * PB:(i + 1) * PB]
+    def samp_start(last):
+        for offset in range(1, NY_DEV):
+            samp_copy(last, offset).start()
+        if last:
+            last_all[gy] = last_send[...]
+        else:
+            samp_all[gy] = samp_send[...]
+
+    def samp_wait(last):
+        for offset in range(1, NY_DEV):
+            samp_copy(last, offset, True).wait_recv()
 
     row = lax.broadcasted_iota(jnp.int32, (8, PB), 0)
+    width = 4 * K_DEV * PB
 
     def entry_rows(i, carry):
         held = []
@@ -496,28 +470,83 @@
                     wanted = jnp.where(row < 4, 2 * k, 2 * k + 1)
                     pieces.append(jnp.where(wanted == target, pair, 0.0))
                 held.append(jnp.concatenate(pieces, axis=0).astype(BF16))
-        width = 4 * K_DEV * PB
         lhs[:, pl.ds(pl.multiple_of(i * width, width), width)] = jnp.concatenate(held, axis=1)
         return carry
 
+    def last_rows():
+        for brick in range(NY_DEV):
+            held = []
+            for i in range(SLOT // PB):
+                block = brick * (SLOT // PB) + i
+                samples = last_all[brick, :, i * PB:(i + 1) * PB]
+                for entry in range(K_DEV):
+                    target = jnp.where(
+                        delay_ref[entry, block] == MAXOFF, dir_ref[entry, block], -1)
+                    held.append(jnp.where(row == target, samples, 0.0))
+            picked = jnp.concatenate(held, axis=1)
+            last_lhs[:, brick * width:(brick + 1) * width] = jnp.concatenate(
+                [picked, jnp.zeros_like(picked)], axis=0).astype(BF16)
+
+    def all_weights():
+        return wv[:ENTRIES].reshape(ENTRIES * PB, DB)
+
+    def corr_copy(last, member):
+        source, target = (last_out, last_in) if last else (corr_out, corr_in)
+        return pltpu.make_async_remote_copy(
+            src_ref=source, dst_ref=target.at[member],
+            send_sem=last_ssem if last else corr_ssem,
+            recv_sem=(last_rsem if last else corr_rsem).at[member],
+            device_id=owner, device_id_type=MESH,
+        )
+
+    def corr_start(last):
+        @pl.when(jnp.logical_not(is_owner))
+        def _():
+            corr_copy(last, group).start()
+
+    far_pairs(0, 28, 14)
+    leap(0)
+    far_pairs(28, PAIRS - 28, 12)
+    core_start()
+    leap(1)
+    sample(0)
+    sample(1)
+    for half in range(2):
+        core_finish(half)
+        ring_begin(half, 0)
+    leap(2)
+    save_prev = pltpu.make_async_copy(
+        field_b.at[pl.ds(1, CX), pl.ds(LOW, CY)], prev_ref, load_sem.at[5])
+    save_prev.start()
+    sample(2)
+    samp_start(0)
+    for half in range(2):
+        ring_forward(half, 0)
+    leap(3)
+    sample(3)
+    samp_start(1)
+    save_next = pltpu.make_async_copy(
+        field_a.at[pl.ds(1, CX), pl.ds(LOW, CY)], next_ref, load_sem.at[6])
+    save_next.start()
+    for half in range(2):
+        first, second = ring_end(half, 0)
+        totals[half, 0:2] = first
+        totals[half, 2:4] = second
+        ring_begin(half, 1)
+    samp_wait(0)
+    for brick in range(NY_DEV):
+        for i in range(SLOT // PB):
+            spad[brick * (SLOT // PB) + i, 32:40, :] = samp_all[brick, :, i * PB:(i + 1) * PB]
     lax.fori_loop(0, BLOCKS // 4, entry_rows, 0)
+    corr_out[...] = jnp.dot(lhs[...], all_weights(), preferred_element_type=F32)
+    corr_start(0)
     for half in range(2):
         ring_forward(half, 1)
-    flat_weights = wv[:ENTRIES].reshape(BLOCKS * K_DEV * PB, DB)
-    correction = jnp.dot(lhs[...], flat_weights, preferred_element_type=F32)
-    corr_out[...] = correction
-
-    def corr_copy(member):
-        return pltpu.make_async_remote_copy(
-            src_ref=corr_out, dst_ref=corr_in.at[member],
-            send_sem=corr_ssem, recv_sem=corr_rsem.at[member],
-            device_id=owner, device_id_type=MESH,
-        )
-
-    @pl.when(jnp.logical_not(is_owner))
-    def _():
-        corr_copy(group).start()
-
+    samp_wait(1)
+    last_rows()
+    last_out[...] = jnp.dot(
+        last_lhs[...], all_weights(), preferred_element_type=F32)[:8]
+    corr_start(1)
     for half in range(2):
         first, second = ring_end(half, 1)
         for j in range(4):
@@ -526,11 +555,13 @@
 
     @pl.when(is_owner)
     def _():
-        def arrive(member, carry):
-            corr_copy(member).wait_recv()
-            return carry
-
-        lax.fori_loop(0, OWNERS - 1, arrive, 0)
+        def arrivals(last):
+            def one(member, carry):
+                corr_copy(last, member).wait_recv()
+                return carry
+            lax.fori_loop(0, OWNERS - 1, one, 0)
+
+        arrivals(0)
         total = corr_out[...]
         for member in range(OWNERS - 1):
             total = total + corr_in[member]
@@ -540,6 +571,13 @@
                 piece = pltpu.roll(piece, 4, 0)
             columns = slice(j * DB, (j + 1) * DB)
             far_ref[8:16, columns] = far_ref[8:16, columns] + jnp.where(row >= 4, piece, 0.0)
+        arrivals(1)
+        total = last_out[...]
+        for member in range(OWNERS - 1):
+            total = total + last_in[member]
+        for j in range(TARGETS):
+            columns = slice(j * DB, (j + 1) * DB)
+            far_ref[15:16, columns] = far_ref[15:16, columns] + total[j:j + 1, :]
 
     for step in range(STEPS):
         halo_wait_send(step, (0, 1, 2) if step == STEPS - 1 else (1, 2))
@@ -549,12 +587,14 @@
             for kind in range(3):
                 for way in range(2):
                     ring_copy(half, stage, kind, way).wait_send()
-    for offset in range(1, NY_DEV):
-        samp_copy(offset).wait_send()
+    for last in range(2):
+        for offset in range(1, NY_DEV):
+            samp_copy(last, offset).wait_send()
 
     @pl.when(jnp.logical_not(is_owner))
     def _():
-        corr_copy(group).wait_send()
+        corr_copy(0, group).wait_send()
+        corr_copy(1, group).wait_send()
 
     save_prev.wait()
     save_next.wait()
@@ -582,11 +622,14 @@
             pltpu.VMEM((STEPS, 2, CX, CZ), F32),
             pltpu.VMEM((STEPS, 2, CY, CZ), F32),
             pltpu.VMEM((CX * CY, SLOT), BF16),
-            pltpu.VMEM((CX * CY, CZ), BF16),
+            pltpu.VMEM((2, CX * CY, CZ), BF16),
+            pltpu.VMEM((8, SLOT), F32),
+            pltpu.VMEM((NY_DEV, 8, SLOT), F32),
             pltpu.VMEM((8, SLOT), F32),
             pltpu.VMEM((NY_DEV, 8, SLOT), F32),
             pltpu.VMEM((BLOCKS, 48, PB), F32),
-            pltpu.VMEM((32, BLOCKS * K_DEV * PB), BF16),
+            pltpu.VMEM((32, ENTRIES * PB), BF16),
+            pltpu.VMEM((16, ENTRIES * PB), BF16),
             pltpu.VMEM((ENTRIES + 1, PB, DB), BF16),
             pltpu.VMEM((BLOCKS, TW + MAXOFF, PB), F32),
             pltpu.VMEM((PAIRS + 1, TW, DB), F32),
@@ -601,12 +644,14 @@
             pltpu.VMEM((2, 3, 2, 2, ROWS, DB), F32),
             pltpu.VMEM((32, DB), F32),
             pltpu.VMEM((OWNERS, 32, DB), F32),
+            pltpu.VMEM((8, DB), F32),
+            pltpu.VMEM((OWNERS, 8, DB), F32),
             dma((8,)),
             dma((STEPS, 3, 2)), dma((STEPS, 3, 2)),
-            dma((3,)), dma((3,)),
+            dma((2, 3)), dma((2, 3)),
             dma((2,)), dma((2,)),
             dma((2, 2, 3, 2)), dma((2, 2, 3, 2)),
-            dma, dma((OWNERS,)),
+            dma, dma((OWNERS,)), dma, dma((OWNERS,)),
         ],
         compiler_params=pltpu.CompilerParams(
             collective_id=0, has_side_effects=True, vmem_limit_bytes=58 * 1024 * 1024),

time: 39.3 us -> 38.6 us (0.982)
  Pallas kernels: 38.5 us -> 37.8 us
    pallas_call x1, Pallas kernels: 36.5 us -> 35.7 us  [hall(): pl.pallas_call(hall_kernel, out_shape=(brick, brick, jax.ShapeDtypeStruct...]
where the time goes in v2:
time: 38.6 us; the launch traced here: 38.4 us
  Pallas kernels  37.8 us (98%)
  between operations  0.64 us (2%)
    pallas_call x1, Pallas kernels, hall(): pl.pallas_call(hall_kernel, out_shape=(brick, brick, jax.ShapeDtypeStruct...  35.7 us
    pallas_call x1, Pallas kernels, save(): pl.pallas_call(save_kernel, out_shape=tuple((jax.ShapeDtypeStruct(a.shape...  2.07 us

profile of v2, /device:TPU:0, one launch (start us, length us, event | category | flops | bytes accessed | tf_op | source)
XLA Modules:
  0.0 38.4 jit_solution(15776438932279919933)
XLA Ops:
  0.6 35.7 %shard_map.103 = (f32[32,32,128]{2,1,0:T(8,128)}, f32[32,32,128]{2,1,0:T(8,128)}, f32[16,1024]{1,0:T(8,128)}) custom-call(s32[6,16]{1,0:T(8,128)} %bitcast.4, s32[6,16]{1,0:T(8,128)} %bitcast.6, s32[6,16]{1,0:T(8,128)} %bitcast.5, s32[1,512]{1,0:T(1,128)} %surf_ref.1, bf16[540,2048]{1,0:T(8,128)(2,1)} %hist_ref.1, f32[32,32,128]{2,1,0:T(8,128)} %now_ref.1, ...), custom_call_target="tpu_custom_call" | custom-call | tf_op jit(solution)/shard_map/pallas_call | solution.py:609
  36.3 2.1 %shard_map.104 = (f32[32,32,128]{2,1,0:T(8,128)}, f32[32,32,128]{2,1,0:T(8,128)}, f32[16,1024]{1,0:T(8,128)}) custom-call(f32[32,32,128]{2,1,0:T(8,128)} %get-tuple-element.6.refs_0_, f32[32,32,128]{2,1,0:T(8,128)} %get-tuple-element.7.refs_1_, f32[16,1024]{1,0:T(8,128)} %get-tuple-element.8.refs_2_), custom_call_target="tpu_custom_call" | custom-call | tf_op jit(solution)/shard_map/pallas_call | solution.py:676

commit v3 on v2

--- a/solution.py
+++ b/solution.py
@@ -309,7 +309,7 @@
     spad[...] = jnp.zeros_like(spad)
     loads[4].wait()
 
-    def leap(step):
+    def leap(step, between=None):
         here_ref, other_ref = fields[step % 2], fields[1 - step % 2]
         last = step == STEPS - 1
         halo_wait_recv(step, (1, 2))
@@ -350,6 +350,8 @@
 
         carry = lax.fori_loop(
             0, (CX - 2) // 10, inner, 0 if last else (zero_plane, zero_plane))
+        if between is not None:
+            between()
         halo_wait_recv(step, (0,))
         if step > 0:
             halo_wait_send(step - 1, (0,))
@@ -509,49 +511,52 @@
     far_pairs(28, PAIRS - 28, 12)
     core_start()
     leap(1)
-    sample(0)
-    sample(1)
     for half in range(2):
         core_finish(half)
         ring_begin(half, 0)
+    sample(0)
+    sample(1)
     leap(2)
     save_prev = pltpu.make_async_copy(
         field_b.at[pl.ds(1, CX), pl.ds(LOW, CY)], prev_ref, load_sem.at[5])
     save_prev.start()
+    for half in range(2):
+        ring_forward(half, 0)
     sample(2)
     samp_start(0)
-    for half in range(2):
-        ring_forward(half, 0)
-    leap(3)
+
+    def second_ring():
+        for half in range(2):
+            first, second = ring_end(half, 0)
+            totals[half, 0:2] = first
+            totals[half, 2:4] = second
+            ring_begin(half, 1)
+
+    leap(3, second_ring)
     sample(3)
     samp_start(1)
     save_next = pltpu.make_async_copy(
         field_a.at[pl.ds(1, CX), pl.ds(LOW, CY)], next_ref, load_sem.at[6])
     save_next.start()
-    for half in range(2):
-        first, second = ring_end(half, 0)
-        totals[half, 0:2] = first
-        totals[half, 2:4] = second
-        ring_begin(half, 1)
     samp_wait(0)
     for brick in range(NY_DEV):
         for i in range(SLOT // PB):
             spad[brick * (SLOT // PB) + i, 32:40, :] = samp_all[brick, :, i * PB:(i + 1) * PB]
     lax.fori_loop(0, BLOCKS // 4, entry_rows, 0)
+    for half in range(2):
+        ring_forward(half, 1)
     corr_out[...] = jnp.dot(lhs[...], all_weights(), preferred_element_type=F32)
     corr_start(0)
     for half in range(2):
-        ring_forward(half, 1)
+        first, second = ring_end(half, 1)
+        for j in range(4):
+            columns = slice((half * 4 + j) * DB, (half * 4 + j + 1) * DB)
+            far_ref[:, columns] = first[j] if j < 2 else second[j - 2]
     samp_wait(1)
     last_rows()
     last_out[...] = jnp.dot(
         last_lhs[...], all_weights(), preferred_element_type=F32)[:8]
     corr_start(1)
-    for half in range(2):
-        first, second = ring_end(half, 1)
-        for j in range(4):
-            columns = slice((half * 4 + j) * DB, (half * 4 + j + 1) * DB)
-            far_ref[:, columns] = first[j] if j < 2 else second[j - 2]
 
     @pl.when(is_owner)
     def _():

time: 38.6 us -> 40.4 us (1.047)
  Pallas kernels: 37.8 us -> 39.6 us
    pallas_call x1, Pallas kernels: 35.7 us -> 37.6 us  [hall(): pl.pallas_call(hall_kernel, out_shape=(brick, brick, jax.ShapeDtypeStruct...]
where the time goes in v3:
time: 40.4 us; the launch traced here: 40.3 us
  Pallas kernels  39.6 us (98%)
  between operations  0.64 us (2%)
    pallas_call x1, Pallas kernels, hall(): pl.pallas_call(hall_kernel, out_shape=(brick, brick, jax.ShapeDtypeStruct...  37.6 us
    pallas_call x1, Pallas kernels, save(): pl.pallas_call(save_kernel, out_shape=tuple((jax.ShapeDtypeStruct(a.shape...  2.07 us

profile of v3, /device:TPU:0, one launch (start us, length us, event | category | flops | bytes accessed | tf_op | source)
XLA Modules:
  0.0 40.3 jit_solution(10521641047193305919)
XLA Ops:
  0.6 37.6 %shard_map.103 = (f32[32,32,128]{2,1,0:T(8,128)}, f32[32,32,128]{2,1,0:T(8,128)}, f32[16,1024]{1,0:T(8,128)}) custom-call(s32[6,16]{1,0:T(8,128)} %bitcast.4, s32[6,16]{1,0:T(8,128)} %bitcast.6, s32[6,16]{1,0:T(8,128)} %bitcast.5, s32[1,512]{1,0:T(1,128)} %surf_ref.1, bf16[540,2048]{1,0:T(8,128)(2,1)} %hist_ref.1, f32[32,32,128]{2,1,0:T(8,128)} %now_ref.1, ...), custom_call_target="tpu_custom_call" | custom-call | tf_op jit(solution)/shard_map/pallas_call | solution.py:614
  38.2 2.1 %shard_map.104 = (f32[32,32,128]{2,1,0:T(8,128)}, f32[32,32,128]{2,1,0:T(8,128)}, f32[16,1024]{1,0:T(8,128)}) custom-call(f32[32,32,128]{2,1,0:T(8,128)} %get-tuple-element.6.refs_0_, f32[32,32,128]{2,1,0:T(8,128)} %get-tuple-element.7.refs_1_, f32[16,1024]{1,0:T(8,128)} %get-tuple-element.8.refs_2_), custom_call_target="tpu_custom_call" | custom-call | tf_op jit(solution)/shard_map/pallas_call | solution.py:681

commit v4 on v2

--- a/solution.py
+++ b/solution.py
@@ -28,8 +28,11 @@
 OWNERS = 32
 ROWS = 16
 NX_DEV, NY_DEV, NZ_DEV = 8, 4, 4
-LOW, HIGH = 8, 40
-PADROWS = 48
+LOW, HIGH = 16, 48
+WIDE_LOW, WIDE_HIGH = 8, 56
+PADROWS = 64
+ROUNDS = 2
+EDGES = [(a, i, b, j) for a, b in ((0, 1), (0, 2), (1, 2)) for i in (0, 1) for j in (0, 1)]
 
 
 def coefficient_table():
@@ -47,13 +50,12 @@
 def hall_kernel(
     dir_ref, delay_ref, dirs_ref, surf_ref, hist_ref, now_ref, old_ref, code_ref, w_ref,
     next_ref, prev_ref, far_ref,
-    field_a, field_b, codes, coef, ystage, zstage, xrecv, yrecv, zrecv,
+    field_a, field_b, codes, coef, stage, land, edges, zlayer, zkeep, zcoef,
     onehot, rounded, samp_send, samp_all, last_send, last_all, spad, lhs, last_lhs, wv,
     signal, trail, table, order, hist, part, core_recv, sums, totals, ring1, ring2, corr_out, corr_in, last_out, last_in,
-    load_sem, halo_send, halo_recv, samp_ssem, samp_rsem,
+    load_sem, halo_send, halo_recv, edge_send, edge_recv, samp_ssem, samp_rsem,
     core_ssem, core_rsem, ring_send, ring_recv, corr_ssem, corr_rsem, last_ssem, last_rsem,
 ):
-    fields = (field_a, field_b)
     gx, gy, gz = lax.axis_index("gx"), lax.axis_index("gy"), lax.axis_index("gz")
     y, z_hi = gx // 2, lax.rem(gx, 2)
     z_lo, core = gz // 2, lax.rem(gz, 2)
@@ -81,6 +83,15 @@
 
     def exists(axis, side):
         return coords[axis] < extents[axis] - 1 if side else coords[axis] > 0
+
+    def across(edge):
+        moved = list(coords)
+        for axis, side in (edge[:2], edge[2:]):
+            moved[axis] = coords[axis] + (1 if side else -1)
+        return tuple(moved)
+
+    def edge_exists(edge):
+        return jnp.logical_and(exists(edge[0], edge[1]), exists(edge[2], edge[3]))
 
     barrier = pltpu.get_barrier_semaphore()
 
@@ -94,6 +105,12 @@
             def _():
                 greet(beside(axis, side))
             expected = expected + exists(axis, side).astype(jnp.int32)
+    for first, i, second, j in EDGES:
+        there = edge_exists((first, i, second, j))
+        @pl.when(there)
+        def _():
+            greet(across((first, i, second, j)))
+        expected = expected + there.astype(jnp.int32)
     greet(sibling)
     for axis in ("y", "z"):
         for offset in (1, 3):
@@ -111,11 +128,11 @@
     expected = expected + jnp.where(is_owner, 0, 1)
 
     loads = [
-        pltpu.make_async_copy(now_ref, field_a.at[pl.ds(1, CX), pl.ds(LOW, CY)], load_sem.at[0]),
+        pltpu.make_async_copy(now_ref, field_a.at[pl.ds(2, CX), pl.ds(LOW, CY)], load_sem.at[0]),
+        pltpu.make_async_copy(old_ref, field_b.at[pl.ds(2, CX), pl.ds(LOW, CY)], load_sem.at[1]),
+        pltpu.make_async_copy(code_ref, codes, load_sem.at[2]),
         pltpu.make_async_copy(hist_ref, hist, load_sem.at[3]),
         pltpu.make_async_copy(w_ref, wv.at[pl.ds(0, ENTRIES)], load_sem.at[4]),
-        pltpu.make_async_copy(code_ref, codes, load_sem.at[2]),
-        pltpu.make_async_copy(old_ref, field_b.at[pl.ds(1, CX), pl.ds(LOW, CY)], load_sem.at[1]),
     ]
     for load in loads:
         load.start()
@@ -128,68 +145,132 @@
             return body([i * unroll + u for u in range(unroll)], carry)
         return lax.fori_loop(0, CX // unroll, chunk, init)
 
-    def take_faces(step, xs, planes, carry):
-        low, high = carry
+    def pack_z(xs, planes, shifts, carry):
         for x, plane in zip(xs, planes):
-            low = jnp.where(lane == x, pltpu.roll(plane, x, 1), low)
-            high = jnp.where(lane == x, pltpu.roll(plane, x + 1, 1), high)
+            carry = [
+                jnp.where(lane == x, pltpu.roll(plane[k], lax.rem(x + shift, CZ), 1), held)
+                for held, (k, shift) in zip(carry, shifts)]
+        return carry
+
+    def pack_now(turn, xs, planes, carry):
+        carry = pack_z(
+            xs, [(p,) for p in planes], ((0, 0), (0, CZ - 1), (0, 1), (0, 2)), carry)
         for x, plane in zip(xs, planes):
-            ystage[step, 0, pl.ds(x, 1), :] = plane[0:1, :]
-            ystage[step, 1, pl.ds(x, 1), :] = plane[CY - 1:CY, :]
-        return low, high
-
-    def halo_copy(step, axis, side):
-        current = step % 2
-        if axis == 0:
-            source = fields[current].at[CX if side else 1, pl.ds(LOW, CY)]
-            target = xrecv.at[step, 1 - side]
-        elif axis == 1:
-            source, target = ystage.at[step, side], yrecv.at[step, 1 - side]
-        else:
-            source, target = zstage.at[step, side], zrecv.at[step, 1 - side]
+            for side, layer, y in ((0, 0, 0), (0, 1, 1), (1, 0, CY - 1), (1, 1, CY - 2)):
+                stage[turn, 1, side, layer, pl.ds(x, 1), :] = plane[y:y + 1, :]
+        return carry
+
+    def pack_now_end(turn, carry):
+        for value, (side, layer) in zip(carry, ((0, 0), (0, 1), (1, 0), (1, 1))):
+            stage[turn, 2, side, layer] = value
+        for side, layer, x in ((0, 0, 0), (0, 1, 1), (1, 0, CX - 1), (1, 1, CX - 2)):
+            stage[turn, 0, side, layer] = field_a[x + 2, LOW:HIGH, :]
+
+    def pack_rest(xs, carry):
+        planes = [(field_b[x + 2, LOW:HIGH, :], codes[x].astype(F32)) for x in xs]
+        carry = pack_z(xs, planes, ((0, 0), (1, 0), (0, 1), (1, 1)), carry)
+        for x, plane in zip(xs, planes):
+            for side, y in ((0, 0), (1, CY - 1)):
+                for k in range(2):
+                    stage[0, 1, side, 2 + k, pl.ds(x, 1), :] = plane[k][y:y + 1, :]
+        return carry
+
+    def pack_rest_end(carry):
+        for value, (side, layer) in zip(carry, ((0, 2), (0, 3), (1, 2), (1, 3))):
+            stage[0, 2, side, layer] = value
+        for side, x in ((0, 0), (1, CX - 1)):
+            stage[0, 0, side, 2] = field_b[x + 2, LOW:HIGH, :]
+            stage[0, 0, side, 3] = codes[x].astype(F32)
+
+    def halo_copy(turn, piece, axis, side):
+        layers = pl.ds(2 * piece, 2)
+        return pltpu.make_async_remote_copy(
+            src_ref=stage.at[turn, axis, side, layers],
+            dst_ref=land.at[turn, axis, 1 - side, layers],
+            send_sem=halo_send.at[turn, piece, axis, side],
+            recv_sem=halo_recv.at[turn, piece, axis, 1 - side],
+            device_id=beside(axis, side), device_id_type=MESH,
+        )
+
+    def edge_copy(turn, edge):
+        a, i, b, j = edge
+        number, opposite = EDGES.index(edge), EDGES.index((a, 1 - i, b, 1 - j))
+        source, target = stage.at[turn, b, j, 0], edges.at[turn, opposite]
+        if (a, b) != (0, 2):
+            source, target = source.at[pl.ds(24 * i, 8)], target.at[pl.ds(0, 8)]
         return pltpu.make_async_remote_copy(
             src_ref=source, dst_ref=target,
-            send_sem=halo_send.at[step, axis, side],
-            recv_sem=halo_recv.at[step, axis, 1 - side],
-            device_id=beside(axis, side), device_id_type=MESH,
+            send_sem=edge_send.at[turn, number], recv_sem=edge_recv.at[turn, opposite],
+            device_id=across(edge), device_id_type=MESH,
         )
 
-    def halo_start(step):
+    def for_faces(act):
         for axis in range(3):
             for side in range(2):
                 @pl.when(exists(axis, side))
                 def _():
-                    halo_copy(step, axis, side).start()
-
-    def halo_wait_send(step, axes=(0, 1, 2)):
-        for axis in axes:
-            for side in range(2):
-                @pl.when(exists(axis, side))
-                def _():
-                    halo_copy(step, axis, side).wait_send()
-
-    def halo_wait_recv(step, axes):
-        for axis in axes:
-            buffer = (xrecv, yrecv, zrecv)[axis]
-            for side in range(2):
-                @pl.when(exists(axis, side))
-                def _():
-                    halo_copy(step, axis, 1 - side).wait_recv()
-                @pl.when(jnp.logical_not(exists(axis, side)))
-                def _():
-                    buffer[step, side] = zero_plane
+                    act(axis, side)
+
+    def for_edges(act):
+        for edge in EDGES:
+            @pl.when(edge_exists(edge))
+            def _():
+                act(edge)
+
+    def halo_start(turn, piece):
+        for_faces(lambda axis, side: halo_copy(turn, piece, axis, side).start())
+        if piece == 0:
+            for_edges(lambda edge: edge_copy(turn, edge).start())
+
+    def halo_wait_recv(turn, piece):
+        for_faces(lambda axis, side: halo_copy(turn, piece, axis, 1 - side).wait_recv())
+        if piece == 0:
+            for_edges(lambda edge: edge_copy(
+                turn, (edge[0], 1 - edge[1], edge[2], 1 - edge[3])).wait_recv())
+
+    def halo_wait_send(turn, piece):
+        for_faces(lambda axis, side: halo_copy(turn, piece, axis, side).wait_send())
+        if piece == 0:
+            for_edges(lambda edge: edge_copy(turn, edge).wait_send())
 
     loads[0].wait()
+    four = [zero_plane] * 4
 
     def first_faces(xs, carry):
-        return take_faces(0, xs, [field_a[x + 1, LOW:HIGH, :] for x in xs], carry)
-
-    low, high = over_planes(first_faces, (zero_plane, zero_plane))
-    zstage[0, 0] = low
-    zstage[0, 1] = high
-
+        return pack_now(0, xs, [field_a[x + 2, LOW:HIGH, :] for x in xs], carry)
+
+    pack_now_end(0, over_planes(first_faces, four))
     pl.semaphore_wait(barrier, expected)
-    halo_start(0)
+    halo_start(0, 0)
+    loads[1].wait()
+    loads[2].wait()
+    pack_rest_end(over_planes(pack_rest, four))
+    halo_start(0, 1)
+
+    for axis in range(3):
+        for side in range(2):
+            @pl.when(jnp.logical_not(exists(axis, side)))
+            def _():
+                land[0, axis, side, 0:3] = jnp.zeros((3, CY, CZ), F32)
+                land[0, axis, side, 3] = jnp.full((CY, CZ), 9.0, F32)
+                land[1, axis, side, 0:2] = jnp.zeros((2, CY, CZ), F32)
+    for number, edge in enumerate(EDGES):
+        @pl.when(jnp.logical_not(edge_exists(edge)))
+        def _():
+            for turn in range(ROUNDS):
+                edges[turn, number] = zero_plane
+
+    for ref in (field_a, field_b):
+        for x in (0, 1, CX + 2, CX + 3):
+            ref[x] = jnp.zeros((PADROWS, CZ), F32)
+        ref[2:CX + 2, 0:LOW, :] = jnp.zeros((CX, LOW, CZ), F32)
+        ref[2:CX + 2, HIGH:, :] = jnp.zeros((CX, PADROWS - HIGH, CZ), F32)
+    zlayer[...] = jnp.zeros_like(zlayer)
+    for index in range(3):
+        for x in (0, CX + 1):
+            coef[index, x] = jnp.zeros((WIDE_HIGH - WIDE_LOW, CZ), F32)
+        coef[index, 1:CX + 1, 0:8, :] = jnp.zeros((CX, 8, CZ), F32)
+        coef[index, 1:CX + 1, 40:48, :] = jnp.zeros((CX, 8, CZ), F32)
 
     dirs = dirs_ref[...]
     targets = jnp.concatenate(
@@ -234,7 +315,7 @@
             device_id=sibling, device_id_type=MESH,
         )
 
-    loads[1].wait()
+    loads[3].wait()
 
     def widen(block, carry):
         signal[block, HOLD:, :] = jnp.zeros((TW + MAXOFF - HOLD, PB), F32)
@@ -245,7 +326,7 @@
         signal[block, :HOLD, :] = hist[:, block * PB:(block + 1) * PB].astype(F32)
     trail[0] = jnp.zeros((TW, DB), F32)
     order_load.wait()
-    loads[2].wait()
+    loads[4].wait()
 
     wv[ENTRIES] = jnp.zeros((PB, DB), BF16)
 
@@ -281,13 +362,11 @@
         for half in range(2):
             core_copy(half).start()
 
-    loads[3].wait()
-
     def plane_coefficients(xs, carry):
         for x in xs:
             code = codes[x]
             for index, values in enumerate(COEFFICIENTS):
-                coef[index, x] = jnp.where(
+                coef[index, x + 1, 8:40, :] = jnp.where(
                     code == 0, values[0],
                     jnp.where(code == 1, values[1], jnp.where(code == 2, values[2], values[3])),
                 ).astype(F32)
@@ -307,58 +386,140 @@
     lax.fori_loop(0, CX * CY // 128, build_onehot, 0)
     samp_send[...] = jnp.zeros_like(samp_send)
     spad[...] = jnp.zeros_like(spad)
-    loads[4].wait()
-
-    def leap(step):
-        here_ref, other_ref = fields[step % 2], fields[1 - step % 2]
-        last = step == STEPS - 1
-        halo_wait_recv(step, (1, 2))
-
-        def y_rows(xs, carry):
-            rows = [(yrecv[step, 0, pl.ds(x, 1), :], yrecv[step, 1, pl.ds(x, 1), :]) for x in xs]
-            for x, (low, high) in zip(xs, rows):
-                here_ref[x + 1, LOW - 1:LOW, :] = low
-                here_ref[x + 1, HIGH:HIGH + 1, :] = high
+
+    def layer_coefficients(code):
+        found = []
+        for values in COEFFICIENTS:
+            value = jnp.zeros_like(code)
+            for number in range(4):
+                value = jnp.where(code == float(number), values[number], value)
+            found.append(value)
+        return found
+
+    def place_rest():
+        halo_wait_recv(0, 1)
+        for side in range(2):
+            x = 1 if side == 0 else CX + 2
+            y = LOW - 1 if side == 0 else HIGH
+            field_b[x, LOW:HIGH, :] = land[0, 0, side, 2]
+            along_x = layer_coefficients(land[0, 0, side, 3])
+            along_y = layer_coefficients(land[0, 1, side, 3])
+            along_z = layer_coefficients(land[0, 2, side, 3])
+            olds = land[0, 1, side, 2]
+            for index in range(3):
+                coef[index, x - 1, 8:40, :] = along_x[index]
+                zcoef[side, index] = along_z[index]
+            for plane in range(CX):
+                field_b[plane + 2, y:y + 1, :] = olds[plane:plane + 1, :]
+                for index in range(3):
+                    coef[index, plane + 1, y - WIDE_LOW:y - WIDE_LOW + 1, :] = (
+                        along_y[index][plane:plane + 1, :])
+
+    def place_now(turn):
+        halo_wait_recv(turn, 0)
+        for side in range(2):
+            for layer in range(2):
+                x = 1 - layer if side == 0 else CX + 2 + layer
+                field_a[x, LOW:HIGH, :] = land[turn, 0, side, layer]
+
+        def rows(xs, carry):
+            held = [
+                [land[turn, 1, side, layer, pl.ds(x, 1), :] for side in (0, 1) for layer in (0, 1)]
+                for x in xs]
+            for x, values in zip(xs, held):
+                for y, value in zip((LOW - 1, LOW - 2, HIGH, HIGH + 1), values):
+                    field_a[x + 2, y:y + 1, :] = value
             return carry
 
-        over_planes(y_rows, 0, 16)
-        z_low, z_high = zrecv[step, 0], zrecv[step, 1]
-
-        def plane_step(xs, carry):
-            planes = []
+        over_planes(rows, 0)
+        for i in range(2):
+            for j in range(2):
+                number = EDGES.index((0, i, 1, j))
+                x, y = (CX + 2 if i else 1), (HIGH if j else LOW - 1)
+                row = 0 if i else 7
+                field_a[x, y:y + 1, :] = edges[turn, number, row:row + 1, :]
+        for side in range(2):
+            face = land[turn, 2, side, 0]
+            below = edges[turn, EDGES.index((0, 0, 2, side))]
+            above = edges[turn, EDGES.index((0, 1, 2, side))]
+            face = jnp.where(lane == CZ - 1, pltpu.roll(below, CZ - CX, 1), face)
+            face = jnp.where(lane == CX, pltpu.roll(above, CX, 1), face)
+            zlayer[side, 8:40, :] = face
+            zlayer[side, 7:8, :] = edges[turn, EDGES.index((1, 0, 2, side)), 7:8, :]
+            zlayer[side, 40:41, :] = edges[turn, EDGES.index((1, 1, 2, side)), 0:1, :]
+
+    def z_neighbours(here, low, high, x):
+        lanes = lax.broadcasted_iota(jnp.int32, here.shape, 1)
+        below = jnp.where(
+            lanes == 0, pltpu.roll(low, lax.rem(CZ - x, CZ), 1), pltpu.roll(here, 1, 1))
+        above = jnp.where(
+            lanes == CZ - 1, pltpu.roll(high, lax.rem(2 * CZ - 1 - x, CZ), 1),
+            pltpu.roll(here, CZ - 1, 1))
+        return below + above
+
+    def keep_rounded(slot, x, values):
+        first = x * CY if isinstance(x, int) else pl.multiple_of(x * CY, CY)
+        rounded[slot, pl.ds(first, CY), :] = values.astype(BF16)
+
+    def wide_step(turn):
+        for side in range(2):
+            here = zlayer[side, 8:40, :]
+            around = pltpu.roll(here, 1, 1) + pltpu.roll(here, CZ - 1, 1)
+            around = around + (zlayer[side, 7:39, :] + zlayer[side, 9:41, :])
+            around = around + (land[turn, 2, side, 1] + stage[turn, 2, side, 0])
+            before = land[0, 2, side, 2] if turn == 0 else zkeep[side]
+            zkeep[side] = (
+                zcoef[side, 0] * here + zcoef[side, 1] * before + zcoef[side, 2] * around)
+        low, high = zlayer[0], zlayer[1]
+
+        def planes(xs):
+            found = []
             for x in xs:
-                here = here_ref[x + 1, LOW:HIGH, :]
-                around = here_ref[x, LOW:HIGH, :] + here_ref[x + 2, LOW:HIGH, :]
+                here = field_a[x + 2, WIDE_LOW:WIDE_HIGH, :]
+                around = (field_a[x + 1, WIDE_LOW:WIDE_HIGH, :]
+                          + field_a[x + 3, WIDE_LOW:WIDE_HIGH, :])
+                around = around + (field_a[x + 2, WIDE_LOW - 1:WIDE_HIGH - 1, :]
+                                   + field_a[x + 2, WIDE_LOW + 1:WIDE_HIGH + 1, :])
+                around = around + z_neighbours(here, low, high, x)
+                before = field_b[x + 2, WIDE_LOW:WIDE_HIGH, :]
+                found.append(
+                    coef[0, x + 1] * here + coef[1, x + 1] * before + coef[2, x + 1] * around)
+            for x, new in zip(xs, found):
+                field_b[x + 2, WIDE_LOW:WIDE_HIGH, :] = new
+            return found
+
+        def inner(xs, carry):
+            for x, new in zip(xs, planes(xs)):
+                keep_rounded(0, x, new[8:40, :])
+            return carry
+
+        over_planes(inner, 0)
+        planes([-1, CX])
+
+    def close_step(turn):
+        low, high = zkeep[0], zkeep[1]
+
+        def planes(xs, carry):
+            found = []
+            for x in xs:
+                here = field_b[x + 2, LOW:HIGH, :]
+                around = field_b[x + 1, LOW:HIGH, :] + field_b[x + 3, LOW:HIGH, :]
                 around = around + (
-                    here_ref[x + 1, LOW - 1:HIGH - 1, :] + here_ref[x + 1, LOW + 1:HIGH + 1, :])
-                below = jnp.where(
-                    lane == 0, pltpu.roll(z_low, lax.rem(CZ - x, CZ), 1), pltpu.roll(here, 1, 1))
-                above = jnp.where(
-                    lane == CZ - 1, pltpu.roll(z_high, CZ - 1 - x, 1), pltpu.roll(here, CZ - 1, 1))
-                around = around + (below + above)
-                before = other_ref[x + 1, LOW:HIGH, :]
-                planes.append(coef[0, x] * here + coef[1, x] * before + coef[2, x] * around)
-            for x, new in zip(xs, planes):
-                other_ref[x + 1, LOW:HIGH, :] = new
-                rounded[step % 2, pl.ds(x * CY if isinstance(x, int) else pl.multiple_of(x * CY, CY), CY), :] = new.astype(BF16)
-            if last:
-                return carry
-            return take_faces(step + 1, xs, planes, carry)
-
-        def inner(i, carry):
-            return plane_step([1 + i * 10 + u for u in range(10)], carry)
-
-        carry = lax.fori_loop(
-            0, (CX - 2) // 10, inner, 0 if last else (zero_plane, zero_plane))
-        halo_wait_recv(step, (0,))
-        if step > 0:
-            halo_wait_send(step - 1, (0,))
-        here_ref[0, LOW:HIGH, :] = xrecv[step, 0]
-        here_ref[CX + 1, LOW:HIGH, :] = xrecv[step, 1]
-        carry = plane_step([0, CX - 1], carry)
-        if not last:
-            zstage[step + 1, 0], zstage[step + 1, 1] = carry
-            halo_start(step + 1)
+                    field_b[x + 2, LOW - 1:HIGH - 1, :] + field_b[x + 2, LOW + 1:HIGH + 1, :])
+                around = around + z_neighbours(here, low, high, x)
+                before = field_a[x + 2, LOW:HIGH, :]
+                found.append(
+                    coef[0, x + 1, 8:40] * here + coef[1, x + 1, 8:40] * before
+                    + coef[2, x + 1, 8:40] * around)
+            for x, new in zip(xs, found):
+                field_a[x + 2, LOW:HIGH, :] = new
+                keep_rounded(1, x, new)
+            return carry if turn else pack_now(1, xs, found, carry)
+
+        carry = over_planes(planes, 0 if turn else four)
+        if turn == 0:
+            pack_now_end(1, carry)
+            halo_start(1, 0)
 
     def sample(step):
         picked = lax.dot_general(
@@ -504,35 +665,32 @@
         def _():
             corr_copy(last, group).start()
 
-    far_pairs(0, 28, 14)
-    leap(0)
-    far_pairs(28, PAIRS - 28, 12)
+    far_pairs(0, PAIRS, 13)
     core_start()
-    leap(1)
+    place_rest()
+    place_now(0)
+    wide_step(0)
+    close_step(0)
     sample(0)
     sample(1)
     for half in range(2):
         core_finish(half)
         ring_begin(half, 0)
-    leap(2)
+    place_now(1)
+    wide_step(1)
     save_prev = pltpu.make_async_copy(
-        field_b.at[pl.ds(1, CX), pl.ds(LOW, CY)], prev_ref, load_sem.at[5])
+        field_b.at[pl.ds(2, CX), pl.ds(LOW, CY)], prev_ref, load_sem.at[5])
     save_prev.start()
+    close_step(1)
+    sample(3)
+    samp_start(1)
     sample(2)
     samp_start(0)
+    save_next = pltpu.make_async_copy(
+        field_a.at[pl.ds(2, CX), pl.ds(LOW, CY)], next_ref, load_sem.at[6])
+    save_next.start()
     for half in range(2):
         ring_forward(half, 0)
-    leap(3)
-    sample(3)
-    samp_start(1)
-    save_next = pltpu.make_async_copy(
-        field_a.at[pl.ds(1, CX), pl.ds(LOW, CY)], next_ref, load_sem.at[6])
-    save_next.start()
-    for half in range(2):
-        first, second = ring_end(half, 0)
-        totals[half, 0:2] = first
-        totals[half, 2:4] = second
-        ring_begin(half, 1)
     samp_wait(0)
     for brick in range(NY_DEV):
         for i in range(SLOT // PB):
@@ -541,12 +699,17 @@
     corr_out[...] = jnp.dot(lhs[...], all_weights(), preferred_element_type=F32)
     corr_start(0)
     for half in range(2):
-        ring_forward(half, 1)
+        first, second = ring_end(half, 0)
+        totals[half, 0:2] = first
+        totals[half, 2:4] = second
+        ring_begin(half, 1)
     samp_wait(1)
     last_rows()
     last_out[...] = jnp.dot(
         last_lhs[...], all_weights(), preferred_element_type=F32)[:8]
     corr_start(1)
+    for half in range(2):
+        ring_forward(half, 1)
     for half in range(2):
         first, second = ring_end(half, 1)
         for j in range(4):
@@ -579,8 +742,8 @@
             columns = slice(j * DB, (j + 1) * DB)
             far_ref[15:16, columns] = far_ref[15:16, columns] + total[j:j + 1, :]
 
-    for step in range(STEPS):
-        halo_wait_send(step, (0, 1, 2) if step == STEPS - 1 else (1, 2))
+    for turn, piece in ((0, 0), (0, 1), (1, 0)):
+        halo_wait_send(turn, piece)
     for half in range(2):
         core_copy(half).wait_send()
         for stage in range(2):
@@ -612,15 +775,16 @@
         in_specs=[smem, smem, vmem, vmem] + [any_space] * 5,
         out_specs=(any_space, any_space, vmem),
         scratch_shapes=[
-            pltpu.VMEM((CX + 2, PADROWS, CZ), F32),
-            pltpu.VMEM((CX + 2, PADROWS, CZ), F32),
+            pltpu.VMEM((CX + 4, PADROWS, CZ), F32),
+            pltpu.VMEM((CX + 4, PADROWS, CZ), F32),
             pltpu.VMEM((CX, CY, CZ), jnp.int32),
-            pltpu.VMEM((3, CX, CY, CZ), F32),
-            pltpu.VMEM((STEPS, 2, CX, CZ), F32),
-            pltpu.VMEM((STEPS, 2, CY, CZ), F32),
-            pltpu.VMEM((STEPS, 2, CY, CZ), F32),
-            pltpu.VMEM((STEPS, 2, CX, CZ), F32),
-            pltpu.VMEM((STEPS, 2, CY, CZ), F32),
+            pltpu.VMEM((3, CX + 2, WIDE_HIGH - WIDE_LOW, CZ), F32),
+            pltpu.VMEM((ROUNDS, 3, 2, 4, CY, CZ), F32),
+            pltpu.VMEM((ROUNDS, 3, 2, 4, CY, CZ), F32),
+            pltpu.VMEM((ROUNDS, len(EDGES), CY, CZ), F32),
+            pltpu.VMEM((2, 48, CZ), F32),
+            pltpu.VMEM((2, CY, CZ), F32),
+            pltpu.VMEM((2, 3, CY, CZ), F32),
             pltpu.VMEM((CX * CY, SLOT), BF16),
             pltpu.VMEM((2, CX * CY, CZ), BF16),
             pltpu.VMEM((8, SLOT), F32),
@@ -647,7 +811,8 @@
             pltpu.VMEM((8, DB), F32),
             pltpu.VMEM((OWNERS, 8, DB), F32),
             dma((8,)),
-            dma((STEPS, 3, 2)), dma((STEPS, 3, 2)),
+            dma((ROUNDS, 2, 3, 2)), dma((ROUNDS, 2, 3, 2)),
+            dma((ROUNDS, len(EDGES))), dma((ROUNDS, len(EDGES))),
             dma((2, 3)), dma((2, 3)),
             dma((2,)), dma((2,)),
             dma((2, 2, 3, 2)), dma((2, 2, 3, 2)),

time: 38.6 us -> 45 us (1.17)
  Pallas kernels: 37.8 us -> 44.2 us
    pallas_call x1, Pallas kernels: 35.7 us -> 42.1 us  [hall(): pl.pallas_call(hall_kernel, out_shape=(brick, brick, jax.ShapeDtypeStruct...]
where the time goes in v4:
time: 45 us; the launch traced here: 44.8 us
  Pallas kernels  44.2 us (98%)
  between operations  0.64 us (1%)
    pallas_call x1, Pallas kernels, hall(): pl.pallas_call(hall_kernel, out_shape=(brick, brick, jax.ShapeDtypeStruct...  42.1 us
    pallas_call x1, Pallas kernels, save(): pl.pallas_call(save_kernel, out_shape=tuple((jax.ShapeDtypeStruct(a.shape...  2.07 us

profile of v4, /device:TPU:0, one launch (start us, length us, event | category | flops | bytes accessed | tf_op | source)
XLA Modules:
  0.0 44.8 jit_solution(12335224496443379400)
XLA Ops:
  0.6 42.1 %shard_map.103 = (f32[32,32,128]{2,1,0:T(8,128)}, f32[32,32,128]{2,1,0:T(8,128)}, f32[16,1024]{1,0:T(8,128)}) custom-call(s32[6,16]{1,0:T(8,128)} %bitcast.4, s32[6,16]{1,0:T(8,128)} %bitcast.6, s32[6,16]{1,0:T(8,128)} %bitcast.5, s32[1,512]{1,0:T(1,128)} %surf_ref.1, bf16[540,2048]{1,0:T(8,128)(2,1)} %hist_ref.1, f32[32,32,128]{2,1,0:T(8,128)} %now_ref.1, ...), custom_call_target="tpu_custom_call" | custom-call | tf_op jit(solution)/shard_map/pallas_call | solution.py:772
  42.8 2.1 %shard_map.104 = (f32[32,32,128]{2,1,0:T(8,128)}, f32[32,32,128]{2,1,0:T(8,128)}, f32[16,1024]{1,0:T(8,128)}) custom-call(f32[32,32,128]{2,1,0:T(8,128)} %get-tuple-element.6.refs_0_, f32[32,32,128]{2,1,0:T(8,128)} %get-tuple-element.7.refs_1_, f32[16,1024]{1,0:T(8,128)} %get-tuple-element.8.refs_2_), custom_call_target="tpu_custom_call" | custom-call | tf_op jit(solution)/shard_map/pallas_call | solution.py:841

commit v5 on v2

--- a/solution.py
+++ b/solution.py
@@ -48,10 +48,10 @@
     dir_ref, delay_ref, dirs_ref, surf_ref, hist_ref, now_ref, old_ref, code_ref, w_ref,
     next_ref, prev_ref, far_ref,
     field_a, field_b, codes, coef, ystage, zstage, xrecv, yrecv, zrecv,
-    onehot, rounded, samp_send, samp_all, last_send, last_all, spad, lhs, last_lhs, wv,
+    onehot, cellmask, rounded, samp_send, samp_all, last_send, last_all, spad, lhs, last_lhs, wv,
     signal, trail, table, order, hist, part, core_recv, sums, totals, ring1, ring2, corr_out, corr_in, last_out, last_in,
     load_sem, halo_send, halo_recv, samp_ssem, samp_rsem,
-    core_ssem, core_rsem, ring_send, ring_recv, corr_ssem, corr_rsem, last_ssem, last_rsem,
+    core_ssem, core_rsem, ring_send, ring_recv, direct_send, direct_recv, corr_ssem, corr_rsem, last_ssem, last_rsem,
 ):
     fields = (field_a, field_b)
     gx, gy, gz = lax.axis_index("gx"), lax.axis_index("gy"), lax.axis_index("gz")
@@ -87,7 +87,7 @@
     def greet(device):
         pl.semaphore_signal(barrier, inc=1, device_id=device, device_id_type=MESH)
 
-    expected = jnp.int32(8)
+    expected = jnp.int32(10)
     for axis in range(3):
         for side in range(2):
             @pl.when(exists(axis, side))
@@ -96,7 +96,7 @@
             expected = expected + exists(axis, side).astype(jnp.int32)
     greet(sibling)
     for axis in ("y", "z"):
-        for offset in (1, 3):
+        for offset in (1, 2, 3):
             greet(ring_neighbour(axis, offset))
     for offset in range(1, NY_DEV):
         greet((gx, lax.rem(gy + offset, NY_DEV), gz))
@@ -128,15 +128,14 @@
             return body([i * unroll + u for u in range(unroll)], carry)
         return lax.fori_loop(0, CX // unroll, chunk, init)
 
-    def take_faces(step, xs, planes, carry):
-        low, high = carry
+    def take_faces(step, xs, planes, held):
         for x, plane in zip(xs, planes):
-            low = jnp.where(lane == x, pltpu.roll(plane, x, 1), low)
-            high = jnp.where(lane == x, pltpu.roll(plane, x + 1, 1), high)
+            mine = jnp.logical_or(lane == 2 * x, lane == lax.rem(2 * x + CZ - 1, CZ))
+            held = jnp.where(mine, pltpu.roll(plane, 2 * x, 1), held)
         for x, plane in zip(xs, planes):
             ystage[step, 0, pl.ds(x, 1), :] = plane[0:1, :]
             ystage[step, 1, pl.ds(x, 1), :] = plane[CY - 1:CY, :]
-        return low, high
+        return held
 
     def halo_copy(step, axis, side):
         current = step % 2
@@ -146,7 +145,7 @@
         elif axis == 1:
             source, target = ystage.at[step, side], yrecv.at[step, 1 - side]
         else:
-            source, target = zstage.at[step, side], zrecv.at[step, 1 - side]
+            source, target = zstage.at[step], zrecv.at[step, 1 - side]
         return pltpu.make_async_remote_copy(
             src_ref=source, dst_ref=target,
             send_sem=halo_send.at[step, axis, side],
@@ -184,9 +183,7 @@
     def first_faces(xs, carry):
         return take_faces(0, xs, [field_a[x + 1, LOW:HIGH, :] for x in xs], carry)
 
-    low, high = over_planes(first_faces, (zero_plane, zero_plane))
-    zstage[0, 0] = low
-    zstage[0, 1] = high
+    zstage[0] = over_planes(first_faces, zero_plane)
 
     pl.semaphore_wait(barrier, expected)
     halo_start(0)
@@ -294,17 +291,16 @@
         return carry
 
     over_planes(plane_coefficients, 0)
-    cell = surf_ref[...]
-    cell_row = lax.shift_right_arithmetic(cell, 7)
-    cell_lane = jnp.bitwise_and(cell, CZ - 1)
-
-    def build_onehot(i, carry):
-        rows = lax.broadcasted_iota(jnp.int32, (128, SLOT), 0) + i * 128
-        onehot[pl.ds(pl.multiple_of(i * 128, 128), 128), :] = jnp.where(
-            rows == cell_row, 1.0, 0.0).astype(BF16)
-        return carry
-
-    lax.fori_loop(0, CX * CY // 128, build_onehot, 0)
+    slot_lane = lax.broadcasted_iota(jnp.int32, (PB, PB), 1)
+    for i in range(SLOT // PB):
+        slots = slice(i * PB, (i + 1) * PB)
+        cell = jnp.broadcast_to(surf_ref[:, slots].astype(F32), (PB, PB)).T.astype(jnp.int32)
+        cell_row = lax.shift_right_arithmetic(cell, 7)
+        cellmask[slots, :] = jnp.where(
+            slot_lane == jnp.bitwise_and(cell, CZ - 1), 1.0, 0.0)
+        for q in range(CX * CY // PB):
+            onehot[slots, q * PB:(q + 1) * PB] = jnp.where(
+                slot_lane + q * PB == cell_row, 1.0, 0.0).astype(BF16)
     samp_send[...] = jnp.zeros_like(samp_send)
     spad[...] = jnp.zeros_like(spad)
     loads[4].wait()
@@ -322,7 +318,10 @@
             return carry
 
         over_planes(y_rows, 0, 16)
-        z_low, z_high = zrecv[step, 0], zrecv[step, 1]
+        z_halo = jnp.where(
+            jnp.bitwise_and(lane, 1) == 0,
+            pltpu.roll(zrecv[step, 0], 1, 1), pltpu.roll(zrecv[step, 1], CZ - 1, 1))
+        ends = jnp.logical_or(lane == 0, lane == CZ - 1)
 
         def plane_step(xs, carry):
             planes = []
@@ -331,11 +330,10 @@
                 around = here_ref[x, LOW:HIGH, :] + here_ref[x + 2, LOW:HIGH, :]
                 around = around + (
                     here_ref[x + 1, LOW - 1:HIGH - 1, :] + here_ref[x + 1, LOW + 1:HIGH + 1, :])
-                below = jnp.where(
-                    lane == 0, pltpu.roll(z_low, lax.rem(CZ - x, CZ), 1), pltpu.roll(here, 1, 1))
-                above = jnp.where(
-                    lane == CZ - 1, pltpu.roll(z_high, CZ - 1 - x, 1), pltpu.roll(here, CZ - 1, 1))
-                around = around + (below + above)
+                beside_z = (jnp.where(lane == 0, 0.0, pltpu.roll(here, 1, 1))
+                            + jnp.where(lane == CZ - 1, 0.0, pltpu.roll(here, CZ - 1, 1)))
+                outside = pltpu.roll(z_halo, lax.rem(2 * (CZ - x), CZ), 1)
+                around = around + (beside_z + jnp.where(ends, outside, 0.0))
                 before = other_ref[x + 1, LOW:HIGH, :]
                 planes.append(coef[0, x] * here + coef[1, x] * before + coef[2, x] * around)
             for x, new in zip(xs, planes):
@@ -349,7 +347,7 @@
             return plane_step([1 + i * 10 + u for u in range(10)], carry)
 
         carry = lax.fori_loop(
-            0, (CX - 2) // 10, inner, 0 if last else (zero_plane, zero_plane))
+            0, (CX - 2) // 10, inner, 0 if last else zero_plane)
         halo_wait_recv(step, (0,))
         if step > 0:
             halo_wait_send(step - 1, (0,))
@@ -357,39 +355,45 @@
         here_ref[CX + 1, LOW:HIGH, :] = xrecv[step, 1]
         carry = plane_step([0, CX - 1], carry)
         if not last:
-            zstage[step + 1, 0], zstage[step + 1, 1] = carry
+            zstage[step + 1] = carry
             halo_start(step + 1)
 
     def sample(step):
-        picked = lax.dot_general(
-            rounded[step % 2], onehot[...], (((0,), (0,)), ((), ())), preferred_element_type=F32)
-        level = lax.broadcasted_iota(jnp.int32, (CZ, SLOT), 0)
-        values = jnp.sum(jnp.where(level == cell_lane, picked, 0.0), axis=0, keepdims=True)
+        picked = jnp.dot(onehot[...], rounded[step % 2], preferred_element_type=F32)
+        values = lax.dot_general(
+            jnp.ones((8, CZ), BF16), (picked * cellmask[...]).astype(BF16),
+            (((1,), (1,)), ((), ())), preferred_element_type=F32)
         if step < STEPS - 1:
-            samp_send[4 + step:5 + step, :] = values
+            samp_send[4 + step:5 + step, :] = values[0:1, :]
         else:
-            last_send[...] = jnp.broadcast_to(values, (8, SLOT))
+            last_send[...] = values
 
     axes = (("z", "y"), ("y", "z"))
 
     def index_on(axis):
         return z if axis == "z" else y
 
-    def ring_copy(half, stage, kind, way):
-        axis = axes[half][stage]
+    def ring_copy(half, kind, way):
+        axis = axes[half][0]
         place_now = index_on(axis)
         step_to = 1 if way == 0 else 3
         chunk = lax.rem(place_now + (2 if kind == 0 else step_to), 4)
-        part = pl.ds(0 if (kind == 1) == (way == 1) else 2, 2)
-        if stage == 0:
-            source, target = sums.at[half, chunk, part], ring1.at[half, kind, way]
-        else:
-            source, target = totals.at[half, chunk, part], ring2.at[half, kind, way]
+        part_now = pl.ds(0 if (kind == 1) == (way == 1) else 2, 2)
         return pltpu.make_async_remote_copy(
-            src_ref=source, dst_ref=target,
-            send_sem=ring_send.at[half, stage, kind, way],
-            recv_sem=ring_recv.at[half, stage, kind, way],
+            src_ref=sums.at[half, chunk, part_now], dst_ref=ring1.at[half, kind, way],
+            send_sem=ring_send.at[half, kind, way],
+            recv_sem=ring_recv.at[half, kind, way],
             device_id=ring_neighbour(axis, step_to), device_id_type=MESH,
+        )
+
+    def direct_copy(half, offset):
+        axis = axes[half][1]
+        return pltpu.make_async_remote_copy(
+            src_ref=totals.at[half, lax.rem(index_on(axis) + offset, 4)],
+            dst_ref=ring2.at[half, offset - 1],
+            send_sem=direct_send.at[half, offset - 1],
+            recv_sem=direct_recv.at[half, offset - 1],
+            device_id=ring_neighbour(axis, offset), device_id_type=MESH,
         )
 
     def core_finish(half):
@@ -404,33 +408,39 @@
                 else:
                     sums[1, yy, zz] = total
 
-    def ring_begin(half, stage):
+    def ring_begin(half):
         for kind in (0, 1):
             for way in (0, 1):
-                ring_copy(half, stage, kind, way).start()
-
-    def ring_forward(half, stage):
-        held = sums if stage == 0 else totals
-        arrived = ring1 if stage == 0 else ring2
-        place_now = index_on(axes[half][stage])
+                ring_copy(half, kind, way).start()
+
+    def ring_forward(half):
+        place_now = index_on(axes[half][0])
         for way in (0, 1):
-            ring_copy(half, stage, 0, way).wait_recv()
+            ring_copy(half, 0, way).wait_recv()
             chunk = lax.rem(place_now + (1 if way == 0 else 3), 4)
             first = 0 if way == 0 else 2
-            held[half, chunk, first:first + 2] = (
-                held[half, chunk, first:first + 2] + arrived[half, 0, way])
-            ring_copy(half, stage, 2, way).start()
-
-    def ring_end(half, stage):
-        held = sums if stage == 0 else totals
-        arrived = ring1 if stage == 0 else ring2
-        place_now = index_on(axes[half][stage])
+            sums[half, chunk, first:first + 2] = (
+                sums[half, chunk, first:first + 2] + ring1[half, 0, way])
+            ring_copy(half, 2, way).start()
+
+    def ring_end(half):
+        place_now = index_on(axes[half][0])
         for kind in (1, 2):
             for way in (0, 1):
-                ring_copy(half, stage, kind, way).wait_recv()
-        first = held[half, place_now, 0:2] + (arrived[half, 2, 0] + arrived[half, 1, 1])
-        second = held[half, place_now, 2:4] + (arrived[half, 1, 0] + arrived[half, 2, 1])
-        return first, second
+                ring_copy(half, kind, way).wait_recv()
+        totals[half, 0:2] = sums[half, place_now, 0:2] + (ring1[half, 2, 0] + ring1[half, 1, 1])
+        totals[half, 2:4] = sums[half, place_now, 2:4] + (ring1[half, 1, 0] + ring1[half, 2, 1])
+        for offset in (2, 1, 3):
+            direct_copy(half, offset).start()
+
+    def direct_end(half):
+        for offset in (1, 2, 3):
+            direct_copy(half, offset).wait_recv()
+        result = totals[half, index_on(axes[half][1])]
+        result = result + (ring2[half, 0] + (ring2[half, 1] + ring2[half, 2]))
+        for j in range(4):
+            columns = slice((half * 4 + j) * DB, (half * 4 + j + 1) * DB)
+            far_ref[:, columns] = result[j]
 
     def samp_copy(last, offset, arriving=False):
         source, target = (last_send, last_all) if last else (samp_send, samp_all)
@@ -513,7 +523,7 @@
     sample(1)
     for half in range(2):
         core_finish(half)
-        ring_begin(half, 0)
+        ring_begin(half)
     leap(2)
     save_prev = pltpu.make_async_copy(
         field_b.at[pl.ds(1, CX), pl.ds(LOW, CY)], prev_ref, load_sem.at[5])
@@ -521,7 +531,7 @@
     sample(2)
     samp_start(0)
     for half in range(2):
-        ring_forward(half, 0)
+        ring_forward(half)
     leap(3)
     sample(3)
     samp_start(1)
@@ -529,10 +539,7 @@
         field_a.at[pl.ds(1, CX), pl.ds(LOW, CY)], next_ref, load_sem.at[6])
     save_next.start()
     for half in range(2):
-        first, second = ring_end(half, 0)
-        totals[half, 0:2] = first
-        totals[half, 2:4] = second
-        ring_begin(half, 1)
+        ring_end(half)
     samp_wait(0)
     for brick in range(NY_DEV):
         for i in range(SLOT // PB):
@@ -540,18 +547,13 @@
     lax.fori_loop(0, BLOCKS // 4, entry_rows, 0)
     corr_out[...] = jnp.dot(lhs[...], all_weights(), preferred_element_type=F32)
     corr_start(0)
-    for half in range(2):
-        ring_forward(half, 1)
     samp_wait(1)
     last_rows()
     last_out[...] = jnp.dot(
         last_lhs[...], all_weights(), preferred_element_type=F32)[:8]
     corr_start(1)
     for half in range(2):
-        first, second = ring_end(half, 1)
-        for j in range(4):
-            columns = slice((half * 4 + j) * DB, (half * 4 + j + 1) * DB)
-            far_ref[:, columns] = first[j] if j < 2 else second[j - 2]
+        direct_end(half)
 
     @pl.when(is_owner)
     def _():
@@ -583,10 +585,11 @@
         halo_wait_send(step, (0, 1, 2) if step == STEPS - 1 else (1, 2))
     for half in range(2):
         core_copy(half).wait_send()
-        for stage in range(2):
-            for kind in range(3):
-                for way in range(2):
-                    ring_copy(half, stage, kind, way).wait_send()
+        for kind in range(3):
+            for way in range(2):
+                ring_copy(half, kind, way).wait_send()
+        for offset in (1, 2, 3):
+            direct_copy(half, offset).wait_send()
     for last in range(2):
         for offset in range(1, NY_DEV):
             samp_copy(last, offset).wait_send()
@@ -617,11 +620,12 @@
             pltpu.VMEM((CX, CY, CZ), jnp.int32),
             pltpu.VMEM((3, CX, CY, CZ), F32),
             pltpu.VMEM((STEPS, 2, CX, CZ), F32),
-            pltpu.VMEM((STEPS, 2, CY, CZ), F32),
+            pltpu.VMEM((STEPS, CY, CZ), F32),
             pltpu.VMEM((STEPS, 2, CY, CZ), F32),
             pltpu.VMEM((STEPS, 2, CX, CZ), F32),
             pltpu.VMEM((STEPS, 2, CY, CZ), F32),
-            pltpu.VMEM((CX * CY, SLOT), BF16),
+            pltpu.VMEM((SLOT, CX * CY), BF16),
+            pltpu.VMEM((SLOT, CZ), F32),
             pltpu.VMEM((2, CX * CY, CZ), BF16),
             pltpu.VMEM((8, SLOT), F32),
             pltpu.VMEM((NY_DEV, 8, SLOT), F32),
@@ -641,7 +645,7 @@
             pltpu.VMEM((2, 4, 4, 4, ROWS, DB), F32),
             pltpu.VMEM((2, 4, 4, ROWS, DB), F32),
             pltpu.VMEM((2, 3, 2, 2, 4, ROWS, DB), F32),
-            pltpu.VMEM((2, 3, 2, 2, ROWS, DB), F32),
+            pltpu.VMEM((2, 3, 4, ROWS, DB), F32),
             pltpu.VMEM((32, DB), F32),
             pltpu.VMEM((OWNERS, 32, DB), F32),
             pltpu.VMEM((8, DB), F32),
@@ -650,7 +654,7 @@
             dma((STEPS, 3, 2)), dma((STEPS, 3, 2)),
             dma((2, 3)), dma((2, 3)),
             dma((2,)), dma((2,)),
-            dma((2, 2, 3, 2)), dma((2, 2, 3, 2)),
+            dma((2, 3, 2)), dma((2, 3, 2)), dma((2, 3)), dma((2, 3)),
             dma, dma((OWNERS,)), dma, dma((OWNERS,)),
         ],
         compiler_params=pltpu.CompilerParams(

time: 38.6 us -> 37.6 us (0.974); the launches traced: 38.4 us -> 36.9 us
  Pallas kernels: 37.8 us -> 36.3 us
    pallas_call x1, Pallas kernels: 35.7 us -> 34.2 us  [hall(): pl.pallas_call(hall_kernel, out_shape=(brick, brick, jax.ShapeDtypeStruct...]
where the time goes in v5:
time: 37.6 us; the launch traced here: 36.9 us
  Pallas kernels  36.3 us (97%)
  between operations  0.64 us (2%)
    pallas_call x1, Pallas kernels, hall(): pl.pallas_call(hall_kernel, out_shape=(brick, brick, jax.ShapeDtypeStruct...  34.2 us
    pallas_call x1, Pallas kernels, save(): pl.pallas_call(save_kernel, out_shape=tuple((jax.ShapeDtypeStruct(a.shape...  2.07 us

profile of v5, /device:TPU:0, one launch (start us, length us, event | category | flops | bytes accessed | tf_op | source)
XLA Modules:
  0.0 36.9 jit_solution(2170493934244480433)
XLA Ops:
  0.6 34.2 %shard_map.103 = (f32[32,32,128]{2,1,0:T(8,128)}, f32[32,32,128]{2,1,0:T(8,128)}, f32[16,1024]{1,0:T(8,128)}) custom-call(s32[6,16]{1,0:T(8,128)} %bitcast.4, s32[6,16]{1,0:T(8,128)} %bitcast.6, s32[6,16]{1,0:T(8,128)} %bitcast.5, s32[1,512]{1,0:T(1,128)} %surf_ref.1, bf16[540,2048]{1,0:T(8,128)(2,1)} %hist_ref.1, f32[32,32,128]{2,1,0:T(8,128)} %now_ref.1, ...), custom_call_target="tpu_custom_call" | custom-call | tf_op jit(solution)/shard_map/pallas_call | solution.py:612
  34.9 2.1 %shard_map.104 = (f32[32,32,128]{2,1,0:T(8,128)}, f32[32,32,128]{2,1,0:T(8,128)}, f32[16,1024]{1,0:T(8,128)}) custom-call(f32[32,32,128]{2,1,0:T(8,128)} %get-tuple-element.6.refs_0_, f32[32,32,128]{2,1,0:T(8,128)} %get-tuple-element.7.refs_1_, f32[16,1024]{1,0:T(8,128)} %get-tuple-element.8.refs_2_), custom_call_target="tpu_custom_call" | custom-call | tf_op jit(solution)/shard_map/pallas_call | solution.py:680

commit v6 on v5

--- a/solution.py
+++ b/solution.py
@@ -291,18 +291,6 @@
         return carry
 
     over_planes(plane_coefficients, 0)
-    slot_lane = lax.broadcasted_iota(jnp.int32, (PB, PB), 1)
-    for i in range(SLOT // PB):
-        slots = slice(i * PB, (i + 1) * PB)
-        cell = jnp.broadcast_to(surf_ref[:, slots].astype(F32), (PB, PB)).T.astype(jnp.int32)
-        cell_row = lax.shift_right_arithmetic(cell, 7)
-        cellmask[slots, :] = jnp.where(
-            slot_lane == jnp.bitwise_and(cell, CZ - 1), 1.0, 0.0)
-        for q in range(CX * CY // PB):
-            onehot[slots, q * PB:(q + 1) * PB] = jnp.where(
-                slot_lane + q * PB == cell_row, 1.0, 0.0).astype(BF16)
-    samp_send[...] = jnp.zeros_like(samp_send)
-    spad[...] = jnp.zeros_like(spad)
     loads[4].wait()
 
     def leap(step):
@@ -514,16 +502,29 @@
         def _():
             corr_copy(last, group).start()
 
-    far_pairs(0, 28, 14)
+    far_pairs(0, 36, 12)
     leap(0)
-    far_pairs(28, PAIRS - 28, 12)
+    far_pairs(36, PAIRS - 36, 16)
     core_start()
     leap(1)
-    sample(0)
-    sample(1)
+
+    slot_lane = lax.broadcasted_iota(jnp.int32, (PB, PB), 1)
+    for i in range(SLOT // PB):
+        slots = slice(i * PB, (i + 1) * PB)
+        cell = jnp.broadcast_to(surf_ref[:, slots].astype(F32), (PB, PB)).T.astype(jnp.int32)
+        cell_row = lax.shift_right_arithmetic(cell, 7)
+        cellmask[slots, :] = jnp.where(
+            slot_lane == jnp.bitwise_and(cell, CZ - 1), 1.0, 0.0)
+        for q in range(CX * CY // PB):
+            onehot[slots, q * PB:(q + 1) * PB] = jnp.where(
+                slot_lane + q * PB == cell_row, 1.0, 0.0).astype(BF16)
+    samp_send[...] = jnp.zeros_like(samp_send)
+    spad[...] = jnp.zeros_like(spad)
     for half in range(2):
         core_finish(half)
         ring_begin(half)
+    sample(0)
+    sample(1)
     leap(2)
     save_prev = pltpu.make_async_copy(
         field_b.at[pl.ds(1, CX), pl.ds(LOW, CY)], prev_ref, load_sem.at[5])
@@ -538,8 +539,6 @@
     save_next = pltpu.make_async_copy(
         field_a.at[pl.ds(1, CX), pl.ds(LOW, CY)], next_ref, load_sem.at[6])
     save_next.start()
-    for half in range(2):
-        ring_end(half)
     samp_wait(0)
     for brick in range(NY_DEV):
         for i in range(SLOT // PB):
@@ -547,6 +546,8 @@
     lax.fori_loop(0, BLOCKS // 4, entry_rows, 0)
     corr_out[...] = jnp.dot(lhs[...], all_weights(), preferred_element_type=F32)
     corr_start(0)
+    for half in range(2):
+        ring_end(half)
     samp_wait(1)
     last_rows()
     last_out[...] = jnp.dot(

time: 37.6 us -> 38.2 us (1.016)
  Pallas kernels: 36.3 us -> 36.9 us
    pallas_call x1, Pallas kernels: 34.2 us -> 34.8 us  [hall(): pl.pallas_call(hall_kernel, out_shape=(brick, brick, jax.ShapeDtypeStruct...]
where the time goes in v6:
time: 38.2 us; the launch traced here: 37.5 us
  Pallas kernels  36.9 us (97%)
  between operations  0.64 us (2%)
    pallas_call x1, Pallas kernels, hall(): pl.pallas_call(hall_kernel, out_shape=(brick, brick, jax.ShapeDtypeStruct...  34.8 us
    pallas_call x1, Pallas kernels, save(): pl.pallas_call(save_kernel, out_shape=tuple((jax.ShapeDtypeStruct(a.shape...  2.07 us

profile of v6, /device:TPU:0, one launch (start us, length us, event | category | flops | bytes accessed | tf_op | source)
XLA Modules:
  0.0 37.5 jit_solution(15903535163402858954)
XLA Ops:
  0.6 34.8 %shard_map.103 = (f32[32,32,128]{2,1,0:T(8,128)}, f32[32,32,128]{2,1,0:T(8,128)}, f32[16,1024]{1,0:T(8,128)}) custom-call(s32[6,16]{1,0:T(8,128)} %bitcast.4, s32[6,16]{1,0:T(8,128)} %bitcast.6, s32[6,16]{1,0:T(8,128)} %bitcast.5, s32[1,512]{1,0:T(1,128)} %surf_ref.1, bf16[540,2048]{1,0:T(8,128)(2,1)} %hist_ref.1, f32[32,32,128]{2,1,0:T(8,128)} %now_ref.1, ...), custom_call_target="tpu_custom_call" | custom-call | tf_op jit(solution)/shard_map/pallas_call | solution.py:613
  35.5 2.1 %shard_map.104 = (f32[32,32,128]{2,1,0:T(8,128)}, f32[32,32,128]{2,1,0:T(8,128)}, f32[16,1024]{1,0:T(8,128)}) custom-call(f32[32,32,128]{2,1,0:T(8,128)} %get-tuple-element.6.refs_0_, f32[32,32,128]{2,1,0:T(8,128)} %get-tuple-element.7.refs_1_, f32[16,1024]{1,0:T(8,128)} %get-tuple-element.8.refs_2_), custom_call_target="tpu_custom_call" | custom-call | tf_op jit(solution)/shard_map/pallas_call | solution.py:681

commit v7 on v5

--- a/solution.py
+++ b/solution.py
@@ -178,16 +178,6 @@
                 def _():
                     buffer[step, side] = zero_plane
 
-    loads[0].wait()
-
-    def first_faces(xs, carry):
-        return take_faces(0, xs, [field_a[x + 1, LOW:HIGH, :] for x in xs], carry)
-
-    zstage[0] = over_planes(first_faces, zero_plane)
-
-    pl.semaphore_wait(barrier, expected)
-    halo_start(0)
-
     dirs = dirs_ref[...]
     targets = jnp.concatenate(
         [dirs[k:k + 1, :] for k in range(K_DEV)]
@@ -231,20 +221,30 @@
             device_id=sibling, device_id_type=MESH,
         )
 
+    samp_send[...] = jnp.zeros_like(samp_send)
+    spad[...] = jnp.zeros_like(spad)
+    trail[0] = jnp.zeros((TW, DB), F32)
+    wv[ENTRIES] = jnp.zeros((PB, DB), BF16)
+    for block in range(BLOCKS):
+        signal[block, HOLD:, :] = jnp.zeros((TW + MAXOFF - HOLD, PB), F32)
+
+    loads[0].wait()
+
+    def first_faces(xs, carry):
+        return take_faces(0, xs, [field_a[x + 1, LOW:HIGH, :] for x in xs], carry)
+
+    zstage[0] = over_planes(first_faces, zero_plane)
+
+    pl.semaphore_wait(barrier, expected)
+    halo_start(0)
+
     loads[1].wait()
 
-    def widen(block, carry):
-        signal[block, HOLD:, :] = jnp.zeros((TW + MAXOFF - HOLD, PB), F32)
-        return carry
-
-    lax.fori_loop(0, BLOCKS, widen, 0)
     for block in range(BLOCKS):
         signal[block, :HOLD, :] = hist[:, block * PB:(block + 1) * PB].astype(F32)
-    trail[0] = jnp.zeros((TW, DB), F32)
     order_load.wait()
     loads[2].wait()
 
-    wv[ENTRIES] = jnp.zeros((PB, DB), BF16)
 
     def far_pair(p):
         windows, blocks = [], []
@@ -301,8 +301,6 @@
         for q in range(CX * CY // PB):
             onehot[slots, q * PB:(q + 1) * PB] = jnp.where(
                 slot_lane + q * PB == cell_row, 1.0, 0.0).astype(BF16)
-    samp_send[...] = jnp.zeros_like(samp_send)
-    spad[...] = jnp.zeros_like(spad)
     loads[4].wait()
 
     def leap(step):
@@ -480,25 +478,34 @@
                     wanted = jnp.where(row < 4, 2 * k, 2 * k + 1)
                     pieces.append(jnp.where(wanted == target, pair, 0.0))
                 held.append(jnp.concatenate(pieces, axis=0).astype(BF16))
-        lhs[:, pl.ds(pl.multiple_of(i * width, width), width)] = jnp.concatenate(held, axis=1)
+        part_rows = pl.ds(pl.multiple_of((i // 2) * 32, 32), 32)
+        columns = pl.ds(pl.multiple_of(lax.rem(i, 2) * width, width), width)
+        lhs[part_rows, columns] = jnp.concatenate(held, axis=1)
         return carry
 
     def last_rows():
-        for brick in range(NY_DEV):
-            held = []
-            for i in range(SLOT // PB):
-                block = brick * (SLOT // PB) + i
-                samples = last_all[brick, :, i * PB:(i + 1) * PB]
-                for entry in range(K_DEV):
-                    target = jnp.where(
-                        delay_ref[entry, block] == MAXOFF, dir_ref[entry, block], -1)
-                    held.append(jnp.where(row == target, samples, 0.0))
-            picked = jnp.concatenate(held, axis=1)
-            last_lhs[:, brick * width:(brick + 1) * width] = jnp.concatenate(
-                [picked, jnp.zeros_like(picked)], axis=0).astype(BF16)
-
-    def all_weights():
-        return wv[:ENTRIES].reshape(ENTRIES * PB, DB)
+        for brick in range(NY_DEV // 2):
+            rows = []
+            for part_of in (brick, brick + NY_DEV // 2):
+                held = []
+                for i in range(SLOT // PB):
+                    block = part_of * (SLOT // PB) + i
+                    samples = last_all[part_of, :, i * PB:(i + 1) * PB]
+                    for entry in range(K_DEV):
+                        target = jnp.where(
+                            delay_ref[entry, block] == MAXOFF, dir_ref[entry, block], -1)
+                        held.append(jnp.where(row == target, samples, 0.0))
+                rows.append(jnp.concatenate(held, axis=1))
+            last_lhs[:, brick * width:(brick + 1) * width] = (
+                jnp.concatenate(rows, axis=0).astype(BF16))
+
+    def times_weights(rows_ref):
+        half = ENTRIES // 2
+        beside_each_other = jnp.concatenate(
+            [wv[:half].reshape(half * PB, DB), wv[half:ENTRIES].reshape(half * PB, DB)], axis=1)
+        product = jnp.dot(rows_ref[...], beside_each_other, preferred_element_type=F32)
+        count_rows = product.shape[0] // 2
+        return product[:count_rows, :DB] + product[count_rows:, DB:]
 
     def corr_copy(last, member):
         source, target = (last_out, last_in) if last else (corr_out, corr_in)
@@ -545,12 +552,11 @@
         for i in range(SLOT // PB):
             spad[brick * (SLOT // PB) + i, 32:40, :] = samp_all[brick, :, i * PB:(i + 1) * PB]
     lax.fori_loop(0, BLOCKS // 4, entry_rows, 0)
-    corr_out[...] = jnp.dot(lhs[...], all_weights(), preferred_element_type=F32)
+    corr_out[...] = times_weights(lhs)
     corr_start(0)
     samp_wait(1)
     last_rows()
-    last_out[...] = jnp.dot(
-        last_lhs[...], all_weights(), preferred_element_type=F32)[:8]
+    last_out[...] = times_weights(last_lhs)
     corr_start(1)
     for half in range(2):
         direct_end(half)
@@ -632,8 +638,8 @@
             pltpu.VMEM((8, SLOT), F32),
             pltpu.VMEM((NY_DEV, 8, SLOT), F32),
             pltpu.VMEM((BLOCKS, 48, PB), F32),
-            pltpu.VMEM((32, ENTRIES * PB), BF16),
-            pltpu.VMEM((16, ENTRIES * PB), BF16),
+            pltpu.VMEM((64, ENTRIES // 2 * PB), BF16),
+            pltpu.VMEM((16, ENTRIES // 2 * PB), BF16),
             pltpu.VMEM((ENTRIES + 1, PB, DB), BF16),
             pltpu.VMEM((BLOCKS, TW + MAXOFF, PB), F32),
             pltpu.VMEM((PAIRS + 1, TW, DB), F32),
@@ -664,8 +670,14 @@
 
 def save_kernel(*refs):
     sources, targets, held, sems = refs[:3], refs[3:6], refs[6:9], refs[9]
-    arrivals = [pltpu.make_async_copy(sources[i], held[i], sems.at[0, i]) for i in range(3)]
-    leaves = [pltpu.make_async_copy(held[i], targets[i], sems.at[1, i]) for i in range(3)]
+    pieces = [(i, slice(first, first + CX // 4)) for first in range(0, CX, CX // 4) for i in (0, 1)]
+    pieces.append((2, slice(0, ROWS)))
+    arrivals, leaves = [], []
+    for number, (i, part) in enumerate(pieces):
+        arrivals.append(pltpu.make_async_copy(
+            sources[i].at[part], held[i].at[part], sems.at[0, number]))
+        leaves.append(pltpu.make_async_copy(
+            held[i].at[part], targets[i].at[part], sems.at[1, number]))
     for copy in arrivals:
         copy.start()
     for arrival, leave in zip(arrivals, leaves):
@@ -683,7 +695,7 @@
         in_specs=[any_space] * 3,
         out_specs=(any_space,) * 3,
         scratch_shapes=[pltpu.VMEM(a.shape, a.dtype) for a in arrays]
-        + [pltpu.SemaphoreType.DMA((2, 3))],
+        + [pltpu.SemaphoreType.DMA((2, 9))],
     )(*arrays)
 
 

time: 37.6 us -> 37.4 us (level)
  no operation moved by 1% of the time
where the time goes in v7:
time: 37.4 us; the launch traced here: 36.9 us
  Pallas kernels  36.3 us (97%)
  between operations  0.64 us (2%)
    pallas_call x1, Pallas kernels, hall(): pl.pallas_call(hall_kernel, out_shape=(brick, brick, jax.ShapeDtypeStruct...  34.1 us
    pallas_call x1, Pallas kernels, save(): pl.pallas_call(save_kernel, out_shape=tuple((jax.ShapeDtypeStruct(a.shape...  2.12 us

profile of v7, /device:TPU:0, one launch (start us, length us, event | category | flops | bytes accessed | tf_op | source)
XLA Modules:
  0.0 36.9 jit_solution(7863609809068711165)
XLA Ops:
  0.6 34.1 %shard_map.103 = (f32[32,32,128]{2,1,0:T(8,128)}, f32[32,32,128]{2,1,0:T(8,128)}, f32[16,1024]{1,0:T(8,128)}) custom-call(s32[6,16]{1,0:T(8,128)} %bitcast.4, s32[6,16]{1,0:T(8,128)} %bitcast.6, s32[6,16]{1,0:T(8,128)} %bitcast.5, s32[1,512]{1,0:T(1,128)} %surf_ref.1, bf16[540,2048]{1,0:T(8,128)(2,1)} %hist_ref.1, f32[32,32,128]{2,1,0:T(8,128)} %now_ref.1, ...), custom_call_target="tpu_custom_call" | custom-call | tf_op jit(solution)/shard_map/pallas_call | solution.py:618
  34.8 2.1 %shard_map.104 = (f32[32,32,128]{2,1,0:T(8,128)}, f32[32,32,128]{2,1,0:T(8,128)}, f32[16,1024]{1,0:T(8,128)}) custom-call(f32[32,32,128]{2,1,0:T(8,128)} %get-tuple-element.6.refs_0_, f32[32,32,128]{2,1,0:T(8,128)} %get-tuple-element.7.refs_1_, f32[16,1024]{1,0:T(8,128)} %get-tuple-element.8.refs_2_), custom_call_target="tpu_custom_call" | custom-call | tf_op jit(solution)/shard_map/pallas_call | solution.py:692

commit v8 on v7

--- a/solution.py
+++ b/solution.py
@@ -50,7 +50,7 @@
     field_a, field_b, codes, coef, ystage, zstage, xrecv, yrecv, zrecv,
     onehot, cellmask, rounded, samp_send, samp_all, last_send, last_all, spad, lhs, last_lhs, wv,
     signal, trail, table, order, hist, part, core_recv, sums, totals, ring1, ring2, corr_out, corr_in, last_out, last_in,
-    load_sem, halo_send, halo_recv, samp_ssem, samp_rsem,
+    load_sem, idle_sem, halo_send, halo_recv, samp_ssem, samp_rsem,
     core_ssem, core_rsem, ring_send, ring_recv, direct_send, direct_recv, corr_ssem, corr_rsem, last_ssem, last_rsem,
 ):
     fields = (field_a, field_b)
@@ -366,6 +366,16 @@
         else:
             last_send[...] = values
 
+    def wait_all_recv(ref, sem):
+        pltpu.make_async_remote_copy(
+            src_ref=ref, dst_ref=ref, send_sem=idle_sem, recv_sem=sem,
+            device_id=sibling, device_id_type=MESH).wait_recv()
+
+    def wait_all_send(ref, sem):
+        pltpu.make_async_remote_copy(
+            src_ref=ref, dst_ref=ref, send_sem=sem, recv_sem=idle_sem,
+            device_id=sibling, device_id_type=MESH).wait_send()
+
     axes = (("z", "y"), ("y", "z"))
 
     def index_on(axis):
@@ -379,8 +389,7 @@
         part_now = pl.ds(0 if (kind == 1) == (way == 1) else 2, 2)
         return pltpu.make_async_remote_copy(
             src_ref=sums.at[half, chunk, part_now], dst_ref=ring1.at[half, kind, way],
-            send_sem=ring_send.at[half, kind, way],
-            recv_sem=ring_recv.at[half, kind, way],
+            send_sem=ring_send, recv_sem=ring_recv.at[0 if kind == 0 else 1],
             device_id=ring_neighbour(axis, step_to), device_id_type=MESH,
         )
 
@@ -389,8 +398,7 @@
         return pltpu.make_async_remote_copy(
             src_ref=totals.at[half, lax.rem(index_on(axis) + offset, 4)],
             dst_ref=ring2.at[half, offset - 1],
-            send_sem=direct_send.at[half, offset - 1],
-            recv_sem=direct_recv.at[half, offset - 1],
+            send_sem=direct_send, recv_sem=direct_recv,
             device_id=ring_neighbour(axis, offset), device_id_type=MESH,
         )
 
@@ -411,41 +419,42 @@
             for way in (0, 1):
                 ring_copy(half, kind, way).start()
 
-    def ring_forward(half):
-        place_now = index_on(axes[half][0])
-        for way in (0, 1):
-            ring_copy(half, 0, way).wait_recv()
-            chunk = lax.rem(place_now + (1 if way == 0 else 3), 4)
-            first = 0 if way == 0 else 2
-            sums[half, chunk, first:first + 2] = (
-                sums[half, chunk, first:first + 2] + ring1[half, 0, way])
-            ring_copy(half, 2, way).start()
-
-    def ring_end(half):
-        place_now = index_on(axes[half][0])
-        for kind in (1, 2):
+    def ring_forward():
+        wait_all_recv(ring1.at[:, 0], ring_recv.at[0])
+        for half in range(2):
+            place_now = index_on(axes[half][0])
             for way in (0, 1):
-                ring_copy(half, kind, way).wait_recv()
-        totals[half, 0:2] = sums[half, place_now, 0:2] + (ring1[half, 2, 0] + ring1[half, 1, 1])
-        totals[half, 2:4] = sums[half, place_now, 2:4] + (ring1[half, 1, 0] + ring1[half, 2, 1])
-        for offset in (2, 1, 3):
-            direct_copy(half, offset).start()
-
-    def direct_end(half):
-        for offset in (1, 2, 3):
-            direct_copy(half, offset).wait_recv()
-        result = totals[half, index_on(axes[half][1])]
-        result = result + (ring2[half, 0] + (ring2[half, 1] + ring2[half, 2]))
-        for j in range(4):
-            columns = slice((half * 4 + j) * DB, (half * 4 + j + 1) * DB)
-            far_ref[:, columns] = result[j]
-
-    def samp_copy(last, offset, arriving=False):
+                chunk = lax.rem(place_now + (1 if way == 0 else 3), 4)
+                first = 0 if way == 0 else 2
+                sums[half, chunk, first:first + 2] = (
+                    sums[half, chunk, first:first + 2] + ring1[half, 0, way])
+                ring_copy(half, 2, way).start()
+
+    def ring_end():
+        wait_all_recv(ring1.at[:, pl.ds(1, 2)], ring_recv.at[1])
+        for half in range(2):
+            place_now = index_on(axes[half][0])
+            totals[half, 0:2] = (
+                sums[half, place_now, 0:2] + (ring1[half, 2, 0] + ring1[half, 1, 1]))
+            totals[half, 2:4] = (
+                sums[half, place_now, 2:4] + (ring1[half, 1, 0] + ring1[half, 2, 1]))
+            for offset in (2, 1, 3):
+                direct_copy(half, offset).start()
+
+    def direct_end():
+        wait_all_recv(ring2, direct_recv)
+        for half in range(2):
+            result = totals[half, index_on(axes[half][1])]
+            result = result + (ring2[half, 0] + (ring2[half, 1] + ring2[half, 2]))
+            for j in range(4):
+                columns = slice((half * 4 + j) * DB, (half * 4 + j + 1) * DB)
+                far_ref[:, columns] = result[j]
+
+    def samp_copy(last, offset):
         source, target = (last_send, last_all) if last else (samp_send, samp_all)
-        slot = lax.rem(gy + NY_DEV - offset, NY_DEV) if arriving else gy
         return pltpu.make_async_remote_copy(
-            src_ref=source, dst_ref=target.at[slot],
-            send_sem=samp_ssem.at[last, offset - 1], recv_sem=samp_rsem.at[last, offset - 1],
+            src_ref=source, dst_ref=target.at[gy],
+            send_sem=samp_ssem.at[last], recv_sem=samp_rsem.at[last],
             device_id=(gx, lax.rem(gy + offset, NY_DEV), gz), device_id_type=MESH,
         )
 
@@ -458,8 +467,7 @@
             samp_all[gy] = samp_send[...]
 
     def samp_wait(last):
-        for offset in range(1, NY_DEV):
-            samp_copy(last, offset, True).wait_recv()
+        wait_all_recv((last_all if last else samp_all).at[pl.ds(0, NY_DEV - 1)], samp_rsem.at[last])
 
     row = lax.broadcasted_iota(jnp.int32, (8, PB), 0)
     width = 4 * K_DEV * PB
@@ -512,7 +520,7 @@
         return pltpu.make_async_remote_copy(
             src_ref=source, dst_ref=target.at[member],
             send_sem=last_ssem if last else corr_ssem,
-            recv_sem=(last_rsem if last else corr_rsem).at[member],
+            recv_sem=last_rsem if last else corr_rsem,
             device_id=owner, device_id_type=MESH,
         )
 
@@ -525,28 +533,34 @@
     leap(0)
     far_pairs(28, PAIRS - 28, 12)
     core_start()
+    halo_wait_send(0, (1, 2))
     leap(1)
     sample(0)
     sample(1)
     for half in range(2):
         core_finish(half)
         ring_begin(half)
+    halo_wait_send(1, (1, 2))
     leap(2)
     save_prev = pltpu.make_async_copy(
         field_b.at[pl.ds(1, CX), pl.ds(LOW, CY)], prev_ref, load_sem.at[5])
     save_prev.start()
     sample(2)
     samp_start(0)
-    for half in range(2):
-        ring_forward(half)
+    ring_forward()
+    halo_wait_send(2, (1, 2))
     leap(3)
     sample(3)
     samp_start(1)
     save_next = pltpu.make_async_copy(
         field_a.at[pl.ds(1, CX), pl.ds(LOW, CY)], next_ref, load_sem.at[6])
     save_next.start()
+    ring_end()
+    halo_wait_send(STEPS - 1)
     for half in range(2):
-        ring_end(half)
+        core_copy(half).wait_send()
+    wait_all_send(ring1, ring_send)
+    wait_all_send(samp_all.at[pl.ds(0, NY_DEV - 1)], samp_ssem.at[0])
     samp_wait(0)
     for brick in range(NY_DEV):
         for i in range(SLOT // PB):
@@ -558,16 +572,13 @@
     last_rows()
     last_out[...] = times_weights(last_lhs)
     corr_start(1)
-    for half in range(2):
-        direct_end(half)
+    direct_end()
 
     @pl.when(is_owner)
     def _():
         def arrivals(last):
-            def one(member, carry):
-                corr_copy(last, member).wait_recv()
-                return carry
-            lax.fori_loop(0, OWNERS - 1, one, 0)
+            held, sem = (last_in, last_rsem) if last else (corr_in, corr_rsem)
+            wait_all_recv(held.at[pl.ds(0, OWNERS - 1)], sem)
 
         arrivals(0)
         total = corr_out[...]
@@ -587,18 +598,8 @@
             columns = slice(j * DB, (j + 1) * DB)
             far_ref[15:16, columns] = far_ref[15:16, columns] + total[j:j + 1, :]
 
-    for step in range(STEPS):
-        halo_wait_send(step, (0, 1, 2) if step == STEPS - 1 else (1, 2))
-    for half in range(2):
-        core_copy(half).wait_send()
-        for kind in range(3):
-            for way in range(2):
-                ring_copy(half, kind, way).wait_send()
-        for offset in (1, 2, 3):
-            direct_copy(half, offset).wait_send()
-    for last in range(2):
-        for offset in range(1, NY_DEV):
-            samp_copy(last, offset).wait_send()
+    wait_all_send(ring2, direct_send)
+    wait_all_send(last_all.at[pl.ds(0, NY_DEV - 1)], samp_ssem.at[1])
 
     @pl.when(jnp.logical_not(is_owner))
     def _():
@@ -656,12 +657,12 @@
             pltpu.VMEM((OWNERS, 32, DB), F32),
             pltpu.VMEM((8, DB), F32),
             pltpu.VMEM((OWNERS, 8, DB), F32),
-            dma((8,)),
+            dma((8,)), dma,
             dma((STEPS, 3, 2)), dma((STEPS, 3, 2)),
-            dma((2, 3)), dma((2, 3)),
             dma((2,)), dma((2,)),
-            dma((2, 3, 2)), dma((2, 3, 2)), dma((2, 3)), dma((2, 3)),
-            dma, dma((OWNERS,)), dma, dma((OWNERS,)),
+            dma((2,)), dma((2,)),
+            dma, dma((2,)), dma, dma,
+            dma, dma, dma, dma,
         ],
         compiler_params=pltpu.CompilerParams(
             collective_id=0, has_side_effects=True, vmem_limit_bytes=58 * 1024 * 1024),

time: 37.4 us -> 36.4 us (0.973)
  Pallas kernels: 36.3 us -> 35.5 us
    pallas_call x1, Pallas kernels: 34.1 us -> 33.4 us  [hall(): pl.pallas_call(hall_kernel, out_shape=(brick, brick, jax.ShapeDtypeStruct...]
where the time goes in v8:
time: 36.4 us; the launch traced here: 36.1 us
  Pallas kernels  35.5 us (98%)
  between operations  0.64 us (2%)
    pallas_call x1, Pallas kernels, hall(): pl.pallas_call(hall_kernel, out_shape=(brick, brick, jax.ShapeDtypeStruct...  33.4 us
    pallas_call x1, Pallas kernels, save(): pl.pallas_call(save_kernel, out_shape=tuple((jax.ShapeDtypeStruct(a.shape...  2.12 us

profile of v8, /device:TPU:0, one launch (start us, length us, event | category | flops | bytes accessed | tf_op | source)
XLA Modules:
  0.0 36.1 jit_solution(7035295053446548510)
XLA Ops:
  0.6 33.4 %shard_map.103 = (f32[32,32,128]{2,1,0:T(8,128)}, f32[32,32,128]{2,1,0:T(8,128)}, f32[16,1024]{1,0:T(8,128)}) custom-call(s32[6,16]{1,0:T(8,128)} %bitcast.4, s32[6,16]{1,0:T(8,128)} %bitcast.6, s32[6,16]{1,0:T(8,128)} %bitcast.5, s32[1,512]{1,0:T(1,128)} %surf_ref.1, bf16[540,2048]{1,0:T(8,128)(2,1)} %hist_ref.1, f32[32,32,128]{2,1,0:T(8,128)} %now_ref.1, ...), custom_call_target="tpu_custom_call" | custom-call | tf_op jit(solution)/shard_map/pallas_call | solution.py:619
  34.0 2.1 %shard_map.104 = (f32[32,32,128]{2,1,0:T(8,128)}, f32[32,32,128]{2,1,0:T(8,128)}, f32[16,1024]{1,0:T(8,128)}) custom-call(f32[32,32,128]{2,1,0:T(8,128)} %get-tuple-element.6.refs_0_, f32[32,32,128]{2,1,0:T(8,128)} %get-tuple-element.7.refs_1_, f32[16,1024]{1,0:T(8,128)} %get-tuple-element.8.refs_2_), custom_call_target="tpu_custom_call" | custom-call | tf_op jit(solution)/shard_map/pallas_call | solution.py:693

commit v9 on v8

--- a/solution.py
+++ b/solution.py
@@ -123,7 +123,7 @@
     lane = lax.broadcasted_iota(jnp.int32, (CY, CZ), 1)
     zero_plane = jnp.zeros((CY, CZ), F32)
 
-    def over_planes(body, init, unroll=8):
+    def over_planes(body, init, unroll=16):
         def chunk(i, carry):
             return body([i * unroll + u for u in range(unroll)], carry)
         return lax.fori_loop(0, CX // unroll, chunk, init)
@@ -266,16 +266,13 @@
             return carry
         lax.fori_loop(0, amount // unroll, chunk, 0)
 
-    def far_collect():
-        for j in range(TARGETS):
-            end = jnp.clip(order[1, j], 0, PAIRS)
-            for quarter in range(4):
-                found = trail[end, quarter * 128:(quarter + 1) * 128, :]
-                part[j, quarter] = found.reshape(4, 2, ROWS, DB)
-
     def core_start():
-        far_collect()
         for half in range(2):
+            for j in range(half * 4, half * 4 + 4):
+                end = jnp.clip(order[1, j], 0, PAIRS)
+                for quarter in range(4):
+                    found = trail[end, quarter * 128:(quarter + 1) * 128, :]
+                    part[j, quarter] = found.reshape(4, 2, ROWS, DB)
             core_copy(half).start()
 
     loads[3].wait()
@@ -342,10 +339,10 @@
             return take_faces(step + 1, xs, planes, carry)
 
         def inner(i, carry):
-            return plane_step([1 + i * 10 + u for u in range(10)], carry)
+            return plane_step([1 + i * 15 + u for u in range(15)], carry)
 
         carry = lax.fori_loop(
-            0, (CX - 2) // 10, inner, 0 if last else zero_plane)
+            0, (CX - 2) // 15, inner, 0 if last else zero_plane)
         halo_wait_recv(step, (0,))
         if step > 0:
             halo_wait_send(step - 1, (0,))
@@ -529,9 +526,9 @@
         def _():
             corr_copy(last, group).start()
 
-    far_pairs(0, 28, 14)
+    far_pairs(0, 26, 26)
     leap(0)
-    far_pairs(28, PAIRS - 28, 12)
+    far_pairs(26, 26, 26)
     core_start()
     halo_wait_send(0, (1, 2))
     leap(1)

time: 36.4 us -> 37.6 us (1.033)
  Pallas kernels: 35.5 us -> 36.4 us
    pallas_call x1, Pallas kernels: 33.4 us -> 34.3 us  [hall(): pl.pallas_call(hall_kernel, out_shape=(brick, brick, jax.ShapeDtypeStruct...]
where the time goes in v9:
time: 37.6 us; the launch traced here: 37.1 us
  Pallas kernels  36.4 us (97%)
  between operations  0.64 us (2%)
    pallas_call x1, Pallas kernels, hall(): pl.pallas_call(hall_kernel, out_shape=(brick, brick, jax.ShapeDtypeStruct...  34.3 us
    pallas_call x1, Pallas kernels, save(): pl.pallas_call(save_kernel, out_shape=tuple((jax.ShapeDtypeStruct(a.shape...  2.12 us

profile of v9, /device:TPU:0, one launch (start us, length us, event | category | flops | bytes accessed | tf_op | source)
XLA Modules:
  0.0 37.1 jit_solution(6375629463057364448)
XLA Ops:
  0.6 34.3 %shard_map.103 = (f32[32,32,128]{2,1,0:T(8,128)}, f32[32,32,128]{2,1,0:T(8,128)}, f32[16,1024]{1,0:T(8,128)}) custom-call(s32[6,16]{1,0:T(8,128)} %bitcast.4, s32[6,16]{1,0:T(8,128)} %bitcast.6, s32[6,16]{1,0:T(8,128)} %bitcast.5, s32[1,512]{1,0:T(1,128)} %surf_ref.1, bf16[540,2048]{1,0:T(8,128)(2,1)} %hist_ref.1, f32[32,32,128]{2,1,0:T(8,128)} %now_ref.1, ...), custom_call_target="tpu_custom_call" | custom-call | tf_op jit(solution)/shard_map/pallas_call | solution.py:616
  35.0 2.1 %shard_map.104 = (f32[32,32,128]{2,1,0:T(8,128)}, f32[32,32,128]{2,1,0:T(8,128)}, f32[16,1024]{1,0:T(8,128)}) custom-call(f32[32,32,128]{2,1,0:T(8,128)} %get-tuple-element.6.refs_0_, f32[32,32,128]{2,1,0:T(8,128)} %get-tuple-element.7.refs_1_, f32[16,1024]{1,0:T(8,128)} %get-tuple-element.8.refs_2_), custom_call_target="tpu_custom_call" | custom-call | tf_op jit(solution)/shard_map/pallas_call | solution.py:690

commit v10 on v9

--- a/solution.py
+++ b/solution.py
@@ -123,7 +123,7 @@
     lane = lax.broadcasted_iota(jnp.int32, (CY, CZ), 1)
     zero_plane = jnp.zeros((CY, CZ), F32)
 
-    def over_planes(body, init, unroll=16):
+    def over_planes(body, init, unroll=8):
         def chunk(i, carry):
             return body([i * unroll + u for u in range(unroll)], carry)
         return lax.fori_loop(0, CX // unroll, chunk, init)
@@ -303,6 +303,7 @@
     def leap(step):
         here_ref, other_ref = fields[step % 2], fields[1 - step % 2]
         last = step == STEPS - 1
+        parity = slice(step % 2 * CZ, (step % 2 + 1) * CZ)
         halo_wait_recv(step, (1, 2))
 
         def y_rows(xs, carry):
@@ -333,16 +334,17 @@
                 planes.append(coef[0, x] * here + coef[1, x] * before + coef[2, x] * around)
             for x, new in zip(xs, planes):
                 other_ref[x + 1, LOW:HIGH, :] = new
-                rounded[step % 2, pl.ds(x * CY if isinstance(x, int) else pl.multiple_of(x * CY, CY), CY), :] = new.astype(BF16)
+                first = x * CY if isinstance(x, int) else pl.multiple_of(x * CY, CY)
+                rounded[pl.ds(first, CY), parity] = new.astype(BF16)
             if last:
                 return carry
             return take_faces(step + 1, xs, planes, carry)
 
         def inner(i, carry):
-            return plane_step([1 + i * 15 + u for u in range(15)], carry)
+            return plane_step([1 + i * 10 + u for u in range(10)], carry)
 
         carry = lax.fori_loop(
-            0, (CX - 2) // 15, inner, 0 if last else zero_plane)
+            0, (CX - 2) // 10, inner, 0 if last else zero_plane)
         halo_wait_recv(step, (0,))
         if step > 0:
             halo_wait_send(step - 1, (0,))
@@ -353,11 +355,19 @@
             zstage[step + 1] = carry
             halo_start(step + 1)
 
-    def sample(step):
-        picked = jnp.dot(onehot[...], rounded[step % 2], preferred_element_type=F32)
-        values = lax.dot_general(
+    def to_row(picked):
+        return lax.dot_general(
             jnp.ones((8, CZ), BF16), (picked * cellmask[...]).astype(BF16),
             (((1,), (1,)), ((), ())), preferred_element_type=F32)
+
+    def sample_first_two():
+        picked = jnp.dot(onehot[...], rounded[...], preferred_element_type=F32)
+        for step in range(2):
+            samp_send[4 + step:5 + step, :] = to_row(picked[:, step * CZ:(step + 1) * CZ])[0:1, :]
+
+    def sample(step):
+        parity = slice(step % 2 * CZ, (step % 2 + 1) * CZ)
+        values = to_row(jnp.dot(onehot[...], rounded[:, parity], preferred_element_type=F32))
         if step < STEPS - 1:
             samp_send[4 + step:5 + step, :] = values[0:1, :]
         else:
@@ -526,14 +536,13 @@
         def _():
             corr_copy(last, group).start()
 
-    far_pairs(0, 26, 26)
+    far_pairs(0, 28, 14)
     leap(0)
-    far_pairs(26, 26, 26)
+    far_pairs(28, PAIRS - 28, 12)
     core_start()
     halo_wait_send(0, (1, 2))
     leap(1)
-    sample(0)
-    sample(1)
+    sample_first_two()
     for half in range(2):
         core_finish(half)
         ring_begin(half)
@@ -630,7 +639,7 @@
             pltpu.VMEM((STEPS, 2, CY, CZ), F32),
             pltpu.VMEM((SLOT, CX * CY), BF16),
             pltpu.VMEM((SLOT, CZ), F32),
-            pltpu.VMEM((2, CX * CY, CZ), BF16),
+            pltpu.VMEM((CX * CY, 2 * CZ), BF16),
             pltpu.VMEM((8, SLOT), F32),
             pltpu.VMEM((NY_DEV, 8, SLOT), F32),
             pltpu.VMEM((8, SLOT), F32),
@@ -668,7 +677,7 @@
 
 def save_kernel(*refs):
     sources, targets, held, sems = refs[:3], refs[3:6], refs[6:9], refs[9]
-    pieces = [(i, slice(first, first + CX // 4)) for first in range(0, CX, CX // 4) for i in (0, 1)]
+    pieces = [(i, slice(0, CX)) for i in (0, 1)]
     pieces.append((2, slice(0, ROWS)))
     arrivals, leaves = [], []
     for number, (i, part) in enumerate(pieces):
@@ -693,7 +702,7 @@
         in_specs=[any_space] * 3,
         out_specs=(any_space,) * 3,
         scratch_shapes=[pltpu.VMEM(a.shape, a.dtype) for a in arrays]
-        + [pltpu.SemaphoreType.DMA((2, 9))],
+        + [pltpu.SemaphoreType.DMA((2, 3))],
     )(*arrays)
 
 

time: 37.6 us -> 36.4 us (0.968)
  Pallas kernels: 36.4 us -> 35.2 us
    pallas_call x1, Pallas kernels: 34.3 us -> 33.2 us  [hall(): pl.pallas_call(hall_kernel, out_shape=(brick, brick, jax.ShapeDtypeStruct...]
where the time goes in v10:
time: 36.4 us; the launch traced here: 35.9 us
  Pallas kernels  35.2 us (97%)
  between operations  0.64 us (2%)
    pallas_call x1, Pallas kernels, hall(): pl.pallas_call(hall_kernel, out_shape=(brick, brick, jax.ShapeDtypeStruct...  33.2 us
    pallas_call x1, Pallas kernels, save(): pl.pallas_call(save_kernel, out_shape=tuple((jax.ShapeDtypeStruct(a.shape...  2.07 us

profile of v10, /device:TPU:0, one launch (start us, length us, event | category | flops | bytes accessed | tf_op | source)
XLA Modules:
  0.0 35.9 jit_solution(3487091255993754229)
XLA Ops:
  0.6 33.2 %shard_map.103 = (f32[32,32,128]{2,1,0:T(8,128)}, f32[32,32,128]{2,1,0:T(8,128)}, f32[16,1024]{1,0:T(8,128)}) custom-call(s32[6,16]{1,0:T(8,128)} %bitcast.4, s32[6,16]{1,0:T(8,128)} %bitcast.6, s32[6,16]{1,0:T(8,128)} %bitcast.5, s32[1,512]{1,0:T(1,128)} %surf_ref.1, bf16[540,2048]{1,0:T(8,128)(2,1)} %hist_ref.1, f32[32,32,128]{2,1,0:T(8,128)} %now_ref.1, ...), custom_call_target="tpu_custom_call" | custom-call | tf_op jit(solution)/shard_map/pallas_call | solution.py:625
  33.8 2.1 %shard_map.104 = (f32[32,32,128]{2,1,0:T(8,128)}, f32[32,32,128]{2,1,0:T(8,128)}, f32[16,1024]{1,0:T(8,128)}) custom-call(f32[32,32,128]{2,1,0:T(8,128)} %get-tuple-element.6.refs_0_, f32[32,32,128]{2,1,0:T(8,128)} %get-tuple-element.7.refs_1_, f32[16,1024]{1,0:T(8,128)} %get-tuple-element.8.refs_2_), custom_call_target="tpu_custom_call" | custom-call | tf_op jit(solution)/shard_map/pallas_call | solution.py:699
